TPU v7x, 32 devices: a whole 2x2x4 slice. The times are simulated.
32 devices in a mesh: dp: 2 (over x), context: 4 (over z), tensor: 4 (over y, core).
Axes of the slice: x: 2, y: 2, z: 4, core: 2. Of those that a mesh axis runs over, the one named last changes fastest.
Arguments:
- tokens: bfloat16 [2, 2048, 2560], P('dp', 'context'), may hold values from -6 to 6
- cotangent: bfloat16 [2, 2048, 2560], P('dp', 'context'), may hold values from -6 to 6
- group_order: int32 [8], replicated, may hold values from 0 to 7, each once
- attn_gain: float32 [2560], replicated, may hold values from 0.25 to 1.75
- query_down: bfloat16 [2560, 768], replicated, may hold values from -0.125 to 0.125
- query_gain: float32 [768], replicated, may hold values from 0.25 to 1.75
- latent_down: bfloat16 [2560, 288], replicated, may hold values from -0.125 to 0.125
- latent_gain: float32 [256], replicated, may hold values from 0.25 to 1.75
- query_up: bfloat16 [768, 3840], P(None, 'tensor'), may hold values from -0.4375 to 0.4375
- latent_up: bfloat16 [256, 5120], P(None, 'tensor'), may hold values from -0.375 to 0.375
- attn_out: bfloat16 [2560, 2560], P('tensor'), may hold values from -4 to 4
- mlp_gain: float32 [2560], replicated, may hold values from 0.25 to 1.75
- gate_proj: bfloat16 [2560, 6400], P(None, 'tensor'), may hold values from -0.125 to 0.125
- up_proj: bfloat16 [2560, 6400], P(None, 'tensor'), may hold values from -0.125 to 0.125
- down_proj: bfloat16 [6400, 2560], P('tensor'), may hold values from -0.875 to 0.875
Outputs:
- layer_out: bfloat16 [2, 2048, 2560], P('dp', 'context')
- token_grad: float32 [2, 2048, 2560], P('dp', 'context')
- attn_gain_grad: float32 [2560], P(('dp', 'context'))
- query_down_grad: float32 [2560, 768], P(('dp', 'context'))
- query_gain_grad: float32 [768], P(('dp', 'context'))
- latent_down_grad: float32 [2560, 288], P(('dp', 'context'))
- latent_gain_grad: float32 [256], P(('dp', 'context'))
- query_up_grad: float32 [768, 3840], P(('dp', 'context'), 'tensor')
- latent_up_grad: float32 [256, 5120], P(('dp', 'context'), 'tensor')
- attn_out_grad: float32 [2560, 2560], P('tensor', ('dp', 'context'))
- mlp_gain_grad: float32 [2560], P(('dp', 'context'))
- gate_proj_grad: float32 [2560, 6400], P(('dp', 'context'), 'tensor')
- up_proj_grad: float32 [2560, 6400], P(('dp', 'context'), 'tensor')
- down_proj_grad: float32 [6400, 2560], P('tensor', ('dp', 'context'))
Inputs may be any that keep to these rules, and one draw needn't show every extreme that they name: group_order is a permutation; the shard of context index c holds, in this order, the blocks group_order[2 c] and group_order[2 c + 1] of 256 consecutive positions of each of its sequences.
All inputs are finite; a program needn't handle non-finite values.
Results may differ from a plain program's by a relative error of at most 0.025.
Values may be sent and summed in bfloat16 or wider, within the bound.
A program may use at most 192 MiB of HBM per device.

v0:
```python
import functools
import math

import jax
import jax.numpy as jnp
from jax import lax
from jax.experimental import pallas as pl
from jax.experimental.pallas import tpu as pltpu
from jax.sharding import PartitionSpec as P

NOPE = 64
ROPE = 32
V_DIM = 64
KV_RANK = 256
HALF = 256
GROUP = 5
CHUNK = 256

EPS = 1e-05
RESIDUAL = 1.4 / math.sqrt(62.0)
SCALE = 1.0 / math.sqrt(NOPE + ROPE)
LOG2E = 1.0 / math.log(2.0)
F32 = jnp.float32
BF16 = jnp.bfloat16


def matmul(left, right):
    return jnp.dot(left, right, preferred_element_type=F32)


def times_transposed(left, right):
    return lax.dot_general(left, right, (((1,), (1,)), ((), ())), preferred_element_type=F32)


def transposed_times(left, right):
    return lax.dot_general(left, right, (((0,), (0,)), ((), ())), preferred_element_type=F32)


MESH = pl.DeviceIdType.MESH


def greet(devices):
    barrier = pltpu.get_barrier_semaphore()
    for device in devices:
        pl.semaphore_signal(barrier, inc=1, device_id=device, device_id_type=MESH)
    pl.semaphore_wait(barrier, len(devices))


def line_of(z, contexts):
    return [{"context": lax.rem(z + by, contexts)} for by in range(1, contexts)]


def front_kernel(
    contexts,
    gains,
    tokens,
    cotangent_h,
    query_down_h,
    latent_down_t,
    query_up_h,
    latent_up_h,
    cos_t,
    sin_t,
    q_t,
    latent,
    latent_t,
    rope_keys,
    rope_keys_t,
    one_inverse,
    query_normed,
    query_inverse,
    query_t,
    cache_t,
    cache_inverse_t,
    one_t,
    feed_t,
    latent_up_t,
    cotangent,
    query_down,
    query_up_t,
    latent_up,
    one,
    low,
    keys,
    far,
    line_sem,
    line_got,
    pair_sem,
    pair_got,
    load_sem,
):
    rows, width = tokens.shape
    loads = [
        pltpu.make_async_copy(src, dst, load_sem.at[i])
        for i, (src, dst) in enumerate(
            [
                (query_down_h, query_down),
                (query_up_h, query_up_t),
                (latent_up_h, latent_up),
                (cotangent_h, cotangent),
            ]
        )
    ]
    for load in loads:
        load.start()
    rank = query_down.shape[1]
    kv = cache_t.shape[0]
    z = lax.axis_index("context")
    t = lax.axis_index("tensor")
    bit = lax.rem(t, 2)
    pair = t + 1 - 2 * bit
    gain_one = slice(0, width)
    gain_query = slice(2 * width, 2 * width + rank)
    gain_latent = slice(2 * width + rank, 2 * width + rank + kv)
    greet([{"tensor": pair}] + line_of(z, contexts))

    @pl.loop(0, rows // 32)
    def _(i):
        r = pl.ds(pl.multiple_of(i * 32, 32), 32)
        value = tokens[r, :].astype(F32)
        inverse = lax.rsqrt(jnp.mean(value * value, axis=-1, keepdims=True) + EPS)
        one_inverse[r, :] = inverse
        one[r, :] = (value * inverse * gains[:, gain_one]).astype(BF16)

    raw = times_transposed(latent_down_t[...], one[...])
    lat = raw[:kv]
    inverse = lax.rsqrt(jnp.mean(lat * lat, axis=0, keepdims=True) + EPS)
    cache_inverse_t[...] = inverse
    lat = lat * inverse
    cache_t[...] = lat.astype(BF16)
    column = jnp.broadcast_to(gains[:, gain_latent], (8, kv)).T[:, 0:1]
    keys[0:kv, :] = (lat * column).astype(BF16)
    first = raw[kv : kv + 16]
    second = raw[kv + 16 :]
    cosine = cos_t[...]
    sine = sin_t[...]
    keys[kv : kv + 16, :] = (first * cosine - second * sine).astype(BF16)
    keys[kv + 16 :, :] = (second * cosine + first * sine).astype(BF16)

    part = keys.shape[0] // 2
    mine = pl.ds(pl.multiple_of(bit * part, 16), part)
    sends = [
        pltpu.make_async_remote_copy(
            src_ref=keys.at[mine],
            dst_ref=far.at[bit, by - 1],
            send_sem=line_sem.at[by - 1],
            recv_sem=line_got.at[by - 1],
            device_id={"context": lax.rem(z + by, contexts)},
            device_id_type=MESH,
        )
        for by in range(1, contexts)
    ]
    for copy in sends:
        copy.start()

    loads[0].wait()
    low[...] = matmul(one[...], query_down[...])

    @pl.loop(0, rows // 32)
    def _(i):
        r = pl.ds(pl.multiple_of(i * 32, 32), 32)
        value = low[r, :]
        inverse = lax.rsqrt(jnp.mean(value * value, axis=-1, keepdims=True) + EPS)
        query_inverse[r, :] = inverse
        value = value * inverse
        query_normed[r, :] = value.astype(BF16)
        low[r, :] = value * gains[:, gain_query]

    query = low[...].astype(BF16)
    query_t[...] = query.T
    heads = q_t.shape[0]
    loads[1].wait()
    for h in range(heads):
        full = times_transposed(query_up_t[h * 96 : (h + 1) * 96, :], query)
        first = full[64:80]
        second = full[80:96]
        q_t[h, 0:64, :] = full[0:64].astype(BF16)
        q_t[h, 64:80, :] = (first * cosine - second * sine).astype(BF16)
        q_t[h, 80:96, :] = (second * cosine + first * sine).astype(BF16)

    for copy in sends:
        copy.wait_recv()
    share = pltpu.make_async_remote_copy(
        src_ref=far.at[bit],
        dst_ref=far.at[bit],
        send_sem=pair_sem,
        recv_sem=pair_got,
        device_id={"tensor": pair},
        device_id_type=MESH,
    )
    share.start()

    loads[2].wait()
    latent_up_t[...] = latent_up[...].T
    loads[3].wait()

    @pl.loop(0, width // 256)
    def _(i):
        lines = pl.ds(pl.multiple_of(i * 256, 256), 256)
        one_t[lines, :] = one[:, lines].T
        feed_t[lines, :] = (RESIDUAL * cotangent[:, lines].astype(F32)).astype(BF16).T

    share.wait_recv()
    latent_t[:, 0:rows] = keys[0:kv, :]
    rope_keys_t[:, 0:rows] = keys[kv:, :]
    for s in range(1, contexts):
        cols = slice(s * rows, (s + 1) * rows)
        latent_t[0:part, cols] = far[0, s - 1]
        latent_t[part:, cols] = far[1, s - 1, 0 : kv - part, :]
        rope_keys_t[:, cols] = far[1, s - 1, kv - part :, :]
    latent[...] = latent_t[...].T
    rope_keys[...] = jnp.concatenate(
        [rope_keys_t[...], jnp.zeros((128 - ROPE, rope_keys_t.shape[1]), BF16)], axis=0
    ).T
    for copy in sends:
        copy.wait_send()
    share.wait_send()


def front(
    contexts,
    gains,
    tokens,
    cotangent,
    query_down,
    latent_down_t,
    query_up_t,
    latent_up,
    cos_t,
    sin_t,
):
    rows, width = tokens.shape
    rank = query_down.shape[1]
    span = latent_down_t.shape[0]
    heads = query_up_t.shape[0] // 96
    kv = span - ROPE
    keys = contexts * rows
    inside = pl.BlockSpec(memory_space=pltpu.VMEM)
    anywhere = pl.BlockSpec(memory_space=pl.ANY)
    sds = jax.ShapeDtypeStruct
    dma = pltpu.SemaphoreType.DMA
    return pl.pallas_call(
        functools.partial(front_kernel, contexts),
        in_specs=[inside] * 2
        + [anywhere] * 2
        + [inside]
        + [anywhere] * 2
        + [inside] * 2,
        out_specs=[inside] * 14,
        out_shape=[
            sds((heads, 96, rows), BF16),
            sds((keys, kv), BF16),
            sds((kv, keys), BF16),
            sds((keys, 128), BF16),
            sds((ROPE, keys), BF16),
            sds((rows, 1), F32),
            sds((rows, rank), BF16),
            sds((rows, 1), F32),
            sds((rank, rows), BF16),
            sds((kv, rows), BF16),
            sds((1, rows), F32),
            sds((width, rows), BF16),
            sds((width, rows), BF16),
            sds(latent_up.shape[::-1], BF16),
        ],
        scratch_shapes=[
            pltpu.VMEM(cotangent.shape, BF16),
            pltpu.VMEM(query_down.shape, BF16),
            pltpu.VMEM(query_up_t.shape, BF16),
            pltpu.VMEM(latent_up.shape, BF16),
            pltpu.VMEM((rows, width), BF16),
            pltpu.VMEM((rows, rank), F32),
            pltpu.VMEM((span, rows), BF16),
            pltpu.VMEM((2, contexts - 1, span // 2, rows), BF16),
            dma((contexts - 1,)),
            dma((contexts - 1,)),
            dma,
            dma,
            dma((4,)),
        ],
        compiler_params=pltpu.CompilerParams(
            collective_id=3, has_side_effects=True, vmem_limit_bytes=60 * 1024 * 1024
        ),
        cost_estimate=pl.CostEstimate(
            flops=2 * rows * width * 1200, bytes_accessed=30 * 1024 * 1024, transcendentals=0
        ),
        name="front",
    )(
        gains,
        tokens,
        cotangent,
        query_down,
        latent_down_t,
        query_up_t,
        latent_up,
        cos_t,
        sin_t,
    )


def load_heads(heads, latent, rope_keys, latent_up, q_t, kcat, q_wide):
    for h in range(heads):
        kcat[h, :, :128] = matmul(latent[...], latent_up[:, h * 128 : (h + 1) * 128]).astype(BF16)
        kcat[h, :, 128:] = rope_keys[...]
        q_wide[h, 0:64, :] = q_t[h, 0:64, :]
        q_wide[h, 64:128, :] = jnp.zeros((64, q_wide.shape[2]), BF16)
        q_wide[h, 128:160, :] = q_t[h, 64:96, :]
        q_wide[h, 160:256, :] = jnp.zeros((96, q_wide.shape[2]), BF16)


def causal():
    key_row = lax.broadcasted_iota(jnp.int32, (HALF, HALF), 0)
    query_col = lax.broadcasted_iota(jnp.int32, (HALF, HALF), 1)
    return key_row <= query_col


def fold(value, op):
    return op(value.reshape(HALF // 8, 8, value.shape[-1]), axis=0)


def forward_kernel(
    heads,
    contexts,
    order,
    q_t,
    latent,
    latent_t,
    rope_keys,
    latent_up,
    latent_up_t,
    joined_t,
    exact_t,
    lse,
    kcat,
    v_t,
    q_wide,
    scores,
    top,
    total,
    acc,
    lies,
):
    z = lax.axis_index("context")
    for i in range(2 * contexts):
        slot = lax.rem(z + contexts - i // 2, contexts)
        lies[order[i]] = slot * (2 * HALF) + (i % 2) * HALF
    load_heads(heads, latent, rope_keys, latent_up, q_t, kcat, q_wide)
    for h in range(heads):
        v_t[h] = matmul(latent_up_t[h * 128 + 64 : (h + 1) * 128, :], latent_t[...]).astype(BF16)
    factor = SCALE * LOG2E
    for block in range(2):
        cols = slice(block * HALF, (block + 1) * HALF)
        position = order[2 * z + block]

        def score(j, masked):
            rows = pl.ds(pl.multiple_of(lies[j], HALF), HALF)
            spot = pl.ds(pl.multiple_of(j * HALF, HALF), HALF)
            for h in range(heads):
                s = matmul(kcat[h, rows, :], q_wide[h, :, cols])
                if masked:
                    s = jnp.where(causal(), s, -1e30)
                scores[h, spot, :] = s
                peak = fold(s, jnp.max)
                top[h] = peak if masked else jnp.maximum(top[h], peak)

        score(position, True)

        @pl.loop(0, position)
        def _(j):
            score(j, False)

        for h in range(heads):
            peak = jnp.max(top[h], axis=0, keepdims=True) * factor
            top[h] = jnp.broadcast_to(peak, (8, HALF))
            total[h] = jnp.zeros((8, HALF), F32)
            acc[h] = jnp.zeros((V_DIM, HALF), F32)

        @pl.loop(0, position + 1)
        def _(j):
            rows = pl.ds(pl.multiple_of(lies[j], HALF), HALF)
            spot = pl.ds(pl.multiple_of(j * HALF, HALF), HALF)
            for h in range(heads):
                p = jnp.exp2(scores[h, spot, :] * factor - top[h, 0:1, :])
                total[h] += fold(p, jnp.sum)
                acc[h] += matmul(v_t[h, :, rows], p.astype(BF16))

        for h in range(heads):
            summed = jnp.sum(total[h], axis=0, keepdims=True)
            out = acc[h] / summed
            joined_t[h * V_DIM : (h + 1) * V_DIM, cols] = out.astype(BF16)
            exact_t[h, :, cols] = out
            lse[h, :, cols] = top[h, 0:1, :] + jnp.log2(summed)


def whole_spec(shape):
    return pl.BlockSpec(shape, lambda g: (0,) * len(shape))


def attention_forward(contexts, order, q_t, latent, latent_t, rope_keys, latent_up, latent_up_t):
    count, _, rows = q_t.shape
    keys = latent.shape[0]
    heads = GROUP
    flops = 2 * count * rows * keys * 384
    return pl.pallas_call(
        functools.partial(forward_kernel, heads, contexts),
        grid=(count // heads,),
        in_specs=[
            pl.BlockSpec(memory_space=pltpu.SMEM),
            pl.BlockSpec((heads, 96, rows), lambda g: (g, 0, 0)),
            whole_spec((keys, KV_RANK)),
            whole_spec((KV_RANK, keys)),
            whole_spec((keys, 128)),
            pl.BlockSpec((KV_RANK, heads * 128), lambda g: (0, g)),
            pl.BlockSpec((heads * 128, KV_RANK), lambda g: (g, 0)),
        ],
        out_specs=[
            pl.BlockSpec((heads * V_DIM, rows), lambda g: (g, 0)),
            pl.BlockSpec((heads, V_DIM, rows), lambda g: (g, 0, 0)),
            pl.BlockSpec((heads, 1, rows), lambda g: (g, 0, 0)),
        ],
        out_shape=[
            jax.ShapeDtypeStruct((count * V_DIM, rows), BF16),
            jax.ShapeDtypeStruct((count, V_DIM, rows), F32),
            jax.ShapeDtypeStruct((count, 1, rows), F32),
        ],
        scratch_shapes=[
            pltpu.VMEM((heads, keys, 256), BF16),
            pltpu.VMEM((heads, V_DIM, keys), BF16),
            pltpu.VMEM((heads, 256, rows), BF16),
            pltpu.VMEM((heads, keys, HALF), F32),
            pltpu.VMEM((heads, 8, HALF), F32),
            pltpu.VMEM((heads, 8, HALF), F32),
            pltpu.VMEM((heads, V_DIM, HALF), F32),
            pltpu.SMEM((keys // HALF,), jnp.int32),
        ],
        compiler_params=pltpu.CompilerParams(vmem_limit_bytes=56 * 1024 * 1024),
        cost_estimate=pl.CostEstimate(
            flops=flops, bytes_accessed=12 * 1024 * 1024, transcendentals=count * rows * keys
        ),
        name="attention_forward",
    )(order, q_t, latent, latent_t, rope_keys, latent_up, latent_up_t)


def cuts(size, step=512):
    count = max(1, size // step)
    edges = [i * step for i in range(count)] + [size]
    return list(zip(edges[:-1], edges[1:]))


def feed_forward_kernel(
    contexts,
    tensors,
    joined_t,
    tokens,
    cotangent,
    gain,
    attn_out_h,
    down_h,
    gate_h,
    up_h,
    feed_t_h,
    branch_o,
    two_o,
    hidden_o,
    dgate_o,
    dup_o,
    feed_o,
    dmiddle_o,
    dbranch_o,
    feed_all_o,
    far_two_o,
    far_dgate_o,
    near_o,
    dmix_t,
    gain_o,
    attn_out,
    down,
    gate_w,
    up_w,
    part,
    final,
    near,
    across,
    dhid,
    two,
    trio,
    feed,
    dmiddle,
    load_sem,
    save_sem,
    send_sem,
    recv_sem,
    pair_sem,
    pair_got,
    line_sem,
    line_got,
    turn_sem,
    turn_got,
    keep_sem,
    give_sem,
    give_got,
):
    rows, width = tokens.shape
    half = width // 2
    t = lax.axis_index("tensor")
    bit = lax.rem(t, 2)
    pair = t + 1 - 2 * bit
    others = [pair]
    step = 2
    while step < tensors:
        others.append(t + step - 2 * step * lax.rem(t // step, 2))
        step *= 2

    loads = [
        pltpu.make_async_copy(src, dst, load_sem.at[i])
        for i, (src, dst) in enumerate(
            [(attn_out_h, attn_out), (down_h, down), (gate_h, gate_w), (up_h, up_w)]
        )
    ]
    for load in loads:
        load.start()

    d = lax.axis_index("dp")
    z = lax.axis_index("context")
    greet([{"tensor": i} for i in others] + line_of(z, contexts) + [{"dp": 1 - d}])

    share = half // contexts

    part_share = share // 2

    def turn(e, by):
        owner = lax.rem(z + by, contexts)
        if by == 0:
            src = feed_t_h.at[pl.ds(pl.multiple_of(e * half + owner * share, 16), share)]
            dst = feed_all_o.at[e * share : (e + 1) * share, 0:rows]
            return pltpu.make_async_copy(src, dst, keep_sem.at[e])
        first = e * half + owner * share + bit * part_share
        src = feed_t_h.at[pl.ds(pl.multiple_of(first, 16), part_share)]
        lines = pl.ds(pl.multiple_of(e * share + bit * part_share, 16), part_share)
        dst = feed_all_o.at[lines, by * rows : (by + 1) * rows]
        return pltpu.make_async_remote_copy(
            src_ref=src,
            dst_ref=dst,
            send_sem=turn_sem.at[e, by - 1],
            recv_sem=turn_got.at[e, by - 1],
            device_id={"context": owner},
            device_id_type=MESH,
        )

    turns = [turn(e, by) for e in range(2) for by in range(contexts)]
    for copy in turns:
        copy.start()

    def to_pair(ref, i):
        return pltpu.make_async_remote_copy(
            src_ref=ref,
            dst_ref=ref,
            send_sem=give_sem.at[i],
            recv_sem=give_got.at[i],
            device_id={"tensor": pair},
            device_id_type=MESH,
        )

    def turn_pair(e):
        lines = pl.ds(pl.multiple_of(e * share + bit * part_share, 16), part_share)
        return to_pair(feed_all_o.at[lines, rows:], e)

    def two_pair(c):
        lines = pl.ds(pl.multiple_of(c * CHUNK + bit * (CHUNK // 2), 16), CHUNK // 2)
        return to_pair(far_two_o.at[lines], 2 + c)

    def send(src, dst, job, kind, c, device):
        return pltpu.make_async_remote_copy(
            src_ref=src,
            dst_ref=dst,
            send_sem=send_sem.at[job, kind, c],
            recv_sem=recv_sem.at[job, kind, c],
            device_id={"tensor": device},
            device_id_type=MESH,
        )

    def span(c):
        return pl.ds(c * CHUNK, CHUNK)

    last = len(others)

    def hop(job, c, kind):
        if kind == 0:
            return send(
                part.at[1 - bit, span(c)], near.at[job, span(c)], job, 0, c, pair
            )
        if kind == last:
            here = final.at[job, bit, span(c)]
            return send(here, here, job, last, c, pair)
        src = near if kind == 1 else across.at[kind - 2]
        return send(
            src.at[job, span(c)], across.at[kind - 1, job, span(c)], job, kind, c, others[kind]
        )

    def reduce_pair(job, c):
        hop(job, c, 0).wait_recv()

        @pl.loop(0, CHUNK // 32)
        def _(i):
            r = pl.ds(pl.multiple_of(c * CHUNK + i * 32, 32), 32)
            near[job, r, :] = (
                near[job, r, :].astype(F32) + part[bit, r, :].astype(F32)
            ).astype(BF16)

        hop(job, c, 1).start()

    def reduce_across(job, c):
        for kind in range(1, last):
            hop(job, c, kind).wait_recv()
            src = near if kind == 1 else across.at[kind - 2]
            ending = kind == last - 1

            @pl.loop(0, CHUNK // 32)
            def _(i):
                r = pl.ds(pl.multiple_of(c * CHUNK + i * 32, 32), 32)
                value = (
                    src[job, r, :].astype(F32) + across[kind - 1, job, r, :].astype(F32)
                ).astype(BF16)
                if ending:
                    final[job, bit, r, :] = value
                else:
                    across[kind - 1, job, r, :] = value

            hop(job, c, kind + 1).start()
        hop(job, c, last).wait_recv()

    def middle_rows(r):
        parts = []
        for h in range(2):
            cols = slice(h * half, (h + 1) * half)
            parts.append(
                tokens[r, cols].astype(F32) + RESIDUAL * final[0, h, r, :].astype(F32)
            )
        square = sum(jnp.sum(p * p, axis=-1, keepdims=True) for p in parts)
        inverse = lax.rsqrt(square * (1.0 / width) + EPS)
        return parts, inverse

    def across_pair(c, kind):
        if kind == 0:
            lines = pl.ds(pl.multiple_of(bit * (CHUNK // 2), 16), CHUNK // 2)
            src = two.at[lines, pl.ds(pl.multiple_of((1 - d) * half, 128), half)]
            lines = pl.ds(pl.multiple_of(c * CHUNK + bit * (CHUNK // 2), 16), CHUNK // 2)
            dst = far_two_o.at[lines]
        else:
            src, dst = trio.at[1, span(c)], far_dgate_o.at[span(c)]
        return pltpu.make_async_remote_copy(
            src_ref=src,
            dst_ref=dst,
            send_sem=pair_sem.at[kind, c],
            recv_sem=pair_got.at[kind, c],
            device_id={"dp": 1 - d},
            device_id_type=MESH,
        )

    def along_line(c, way):
        return pltpu.make_async_remote_copy(
            src_ref=trio.at[0, span(c)],
            dst_ref=near_o.at[way, span(c)],
            send_sem=line_sem.at[way, c],
            recv_sem=line_got.at[way, c],
            device_id={"context": z + 1 - 2 * way},
            device_id_type=MESH,
        )

    chunks = rows // CHUNK
    loads[0].wait()
    for c in range(chunks):
        left = joined_t[:, c * CHUNK : (c + 1) * CHUNK]

        for turn_of in range(2):
            side = 1 - bit if turn_of == 0 else bit

            @pl.loop(0, half // 256)
            def _(n):
                cols = pl.ds(pl.multiple_of(side * half + n * 256, 256), 256)
                place = pl.ds(pl.multiple_of(n * 256, 256), 256)
                part[side, span(c), place] = transposed_times(left, attn_out[:, cols]).astype(BF16)

            if turn_of == 0:
                hop(0, c, 0).start()
    for c in range(chunks):
        reduce_pair(0, c)

    loads[1].wait()
    for c in range(chunks):

        @pl.loop(0, CHUNK // 32)
        def _(i):
            r = pl.ds(pl.multiple_of(c * CHUNK + i * 32, 32), 32)
            o = pl.ds(pl.multiple_of(i * 32, 32), 32)
            two[o, :] = (RESIDUAL * cotangent[r, :].astype(F32)).astype(BF16)

        for a, b in cuts(down.shape[0]):
            dhid[span(c), a:b] = times_transposed(two[...], down[a:b, :]).astype(BF16)

    loads[2].wait()
    loads[3].wait()
    saves = []

    def save(src, dst):
        copy = pltpu.make_async_copy(src, dst, save_sem.at[len(saves)])
        copy.start()
        saves.append(copy)
        return copy

    two_saved = None
    for c in range(chunks):
        reduce_across(0, c)
        if c > 0:
            reduce_pair(1, c - 1)
        if two_saved is not None:
            two_saved.wait()
            across_pair(c - 1, 0).wait_send()

        @pl.loop(0, CHUNK // 32)
        def _(i):
            r = pl.ds(pl.multiple_of(c * CHUNK + i * 32, 32), 32)
            o = pl.ds(pl.multiple_of(i * 32, 32), 32)
            parts, inverse = middle_rows(r)
            for h in range(2):
                cols = slice(h * half, (h + 1) * half)
                two[o, cols] = (parts[h] * inverse * gain[:, width + h * half : width + (h + 1) * half]).astype(BF16)

        two_saved = save(two, two_o.at[span(c)])
        across_pair(c, 0).start()
        for a, b in cuts(gate_w.shape[0]):
            gate = times_transposed(two[...], gate_w[a:b, :])
            upper = times_transposed(two[...], up_w[a:b, :])
            grad = dhid[span(c), a:b].astype(F32)
            sigma = 1.0 / (1.0 + jnp.exp(-gate))
            act = gate * sigma
            trio[0, span(c), a:b] = (act * upper).astype(BF16)
            trio[1, span(c), a:b] = (
                grad * upper * sigma * (1.0 + gate * (1.0 - sigma))
            ).astype(BF16)
            trio[2, span(c), a:b] = (grad * act).astype(BF16)
        for k, out in enumerate((hidden_o, dgate_o, dup_o)):
            save(trio.at[k, span(c)], out.at[span(c)])
        across_pair(c, 1).start()

        @pl.when(z < contexts - 1)
        def _():
            along_line(c, 0).start()

        @pl.when(z > 0)
        def _():
            along_line(c, 1).start()

        hop(0, c, 0).wait_send()

        for turn_of in range(2):
            side = 1 - bit if turn_of == 0 else bit

            @pl.loop(0, half // 256)
            def _(n):
                cols = pl.ds(pl.multiple_of(side * half + n * 256, 256), 256)
                place = pl.ds(pl.multiple_of(n * 256, 256), 256)
                value = matmul(trio[1, span(c), :], gate_w[:, cols])
                value += matmul(trio[2, span(c), :], up_w[:, cols])
                part[side, span(c), place] = value.astype(BF16)

            if turn_of == 0:
                hop(1, c, 0).start()
    reduce_pair(1, chunks - 1)
    two_saved.wait()

    for e in range(2):
        for by in range(1, contexts):
            turns[e * contexts + by].wait_recv()
        turn_pair(e).start()
    for c in range(chunks):
        across_pair(c, 0).wait_recv()
        two_pair(c).start()

    gain_o[...] = jnp.zeros_like(gain_o)
    feed_saved = dmiddle_saved = dbranch_saved = None
    for c in range(chunks):
        if feed_saved is not None:
            feed_saved.wait()

        @pl.loop(0, width // 256)
        def _(n):
            cols = pl.ds(pl.multiple_of(n * 256, 256), 256)
            feed[:, cols] = matmul(trio[0, span(c), :], down[:, cols]).astype(BF16)

        feed_saved = save(feed, feed_o.at[span(c)])
        reduce_across(1, c)
        if dmiddle_saved is not None:
            dmiddle_saved.wait()
            dbranch_saved.wait()
        else:
            across_pair(chunks - 1, 0).wait_send()

        @pl.loop(0, CHUNK // 32)
        def _(i):
            r = pl.ds(pl.multiple_of(c * CHUNK + i * 32, 32), 32)
            o = pl.ds(pl.multiple_of(i * 32, 32), 32)
            parts, inverse = middle_rows(r)
            dot = jnp.zeros((32, 1), F32)
            for h in range(2):
                cols = slice(h * half, (h + 1) * half)
                product = final[1, h, r, :].astype(F32) * (parts[h] * inverse)
                gain_o[:, cols] += jnp.sum(product.reshape(4, 8, half), axis=0)
                dot += jnp.sum(product * gain[:, width + h * half : width + (h + 1) * half], axis=-1, keepdims=True)
            dot = dot * (1.0 / width)
            for h in range(2):
                cols = slice(h * half, (h + 1) * half)
                weighted = final[1, h, r, :].astype(F32) * gain[:, width + h * half : width + (h + 1) * half]
                value = cotangent[r, cols].astype(F32) + inverse * (
                    weighted - parts[h] * inverse * dot
                )
                dmiddle[o, cols] = value
                two[o, cols] = (RESIDUAL * value).astype(BF16)

        dmiddle_saved = save(dmiddle, dmiddle_o.at[span(c)])
        dbranch_saved = save(two, dbranch_o.at[span(c)])
        dmix_t[:, c * CHUNK : (c + 1) * CHUNK] = times_transposed(attn_out[...], two[...]).astype(
            BF16
        )
    for h in range(2):
        save(final.at[0, h], branch_o.at[:, h * half : (h + 1) * half])
    for copy in saves[-2:] + [feed_saved, dmiddle_saved, dbranch_saved]:
        copy.wait()
    for e in range(2):
        turns[e * contexts].wait()
        for by in range(1, contexts):
            turns[e * contexts + by].wait_send()
        turn_pair(e).wait()
    for c in range(chunks):
        for k in range(3):
            saves[c * 4 + 1 + k].wait()
    for c in range(chunks):
        two_pair(c).wait()
        across_pair(c, 1).wait()

        @pl.when(z < contexts - 1)
        def _():
            along_line(c, 0).wait_send()
            along_line(c, 1).wait_recv()

        @pl.when(z > 0)
        def _():
            along_line(c, 1).wait_send()
            along_line(c, 0).wait_recv()

    for job in range(2):
        for c in range(chunks):
            for kind in range(1 - job, last + 1):
                hop(job, c, kind).wait_send()


def feed_forward(contexts, tensors, joined_t, tokens, cotangent, gain, attn_out, down, gate_w, up_w, feed_t):
    rows, width = tokens.shape
    units = down.shape[0]
    chunks = rows // CHUNK
    hops = tensors.bit_length() - 1
    anywhere = pl.BlockSpec(memory_space=pl.ANY)
    inside = pl.BlockSpec(memory_space=pltpu.VMEM)
    return pl.pallas_call(
        functools.partial(feed_forward_kernel, contexts, tensors),
        in_specs=[inside] * 4 + [anywhere] * 5,
        out_specs=[anywhere] * 12 + [inside] * 2,
        out_shape=[
            jax.ShapeDtypeStruct((rows, width), BF16),
            jax.ShapeDtypeStruct((rows, width), BF16),
            jax.ShapeDtypeStruct((rows, units), BF16),
            jax.ShapeDtypeStruct((rows, units), BF16),
            jax.ShapeDtypeStruct((rows, units), BF16),
            jax.ShapeDtypeStruct((rows, width), BF16),
            jax.ShapeDtypeStruct((rows, width), F32),
            jax.ShapeDtypeStruct((rows, width), BF16),
            jax.ShapeDtypeStruct((width // contexts, contexts * rows), BF16),
            jax.ShapeDtypeStruct((rows, width // 2), BF16),
            jax.ShapeDtypeStruct((rows, units), BF16),
            jax.ShapeDtypeStruct((2, rows, units), BF16),
            jax.ShapeDtypeStruct((joined_t.shape[0], rows), BF16),
            jax.ShapeDtypeStruct((8, width), F32),
        ],
        scratch_shapes=[
            pltpu.VMEM(attn_out.shape, BF16),
            pltpu.VMEM(down.shape, BF16),
            pltpu.VMEM(gate_w.shape, BF16),
            pltpu.VMEM(up_w.shape, BF16),
            pltpu.VMEM((2, rows, width // 2), BF16),
            pltpu.VMEM((2, 2, rows, width // 2), BF16),
            pltpu.VMEM((2, rows, width // 2), BF16),
            pltpu.VMEM((hops - 1, 2, rows, width // 2), BF16),
            pltpu.VMEM((rows, units), BF16),
            pltpu.VMEM((CHUNK, width), BF16),
            pltpu.VMEM((3, rows, units), BF16),
            pltpu.VMEM((CHUNK, width), BF16),
            pltpu.VMEM((CHUNK, width), F32),
            pltpu.SemaphoreType.DMA((4,)),
            pltpu.SemaphoreType.DMA((7 * chunks + 2,)),
            pltpu.SemaphoreType.DMA((2, hops + 1, chunks)),
            pltpu.SemaphoreType.DMA((2, hops + 1, chunks)),
        ]
        + [pltpu.SemaphoreType.DMA((2, chunks))] * 4
        + [pltpu.SemaphoreType.DMA((2, contexts - 1))] * 2
        + [pltpu.SemaphoreType.DMA((2,))]
        + [pltpu.SemaphoreType.DMA((2 + chunks,))] * 2,
        compiler_params=pltpu.CompilerParams(
            collective_id=0, has_side_effects=True, vmem_limit_bytes=63 * 1024 * 1024
        ),
        cost_estimate=pl.CostEstimate(
            flops=2 * rows * width * units * 6, bytes_accessed=60 * 1024 * 1024, transcendentals=0
        ),
        name="feed_forward",
    )(joined_t, tokens, cotangent, gain, attn_out, down, gate_w, up_w, feed_t)


def backward_kernel(
    contexts,
    group,
    order,
    q_t,
    latent,
    latent_t,
    rope_keys,
    rope_keys_t,
    latent_up,
    latent_up_t,
    exact_t,
    lse,
    dmix_t,
    cos_t,
    sin_t,
    joined_t,
    two_h,
    far_two_h,
    dgate_h,
    far_dgate_h,
    dup_h,
    near_h,
    dbranch_h,
    dq_t,
    grad_up,
    dlat_t,
    gate_o,
    up_o,
    out_o,
    far_out_o,
    far_dup_o,
    spread_o,
    kcat,
    k_t,
    q_wide,
    dmix_wide,
    q_nat,
    dmix_nat,
    delta,
    dq,
    pair,
    lat_acc,
    rope_acc,
    two,
    act,
    gate_w,
    up_w,
    arrived,
    up_arrived,
    out_w,
    joined,
    load_sem,
    dup_sem,
    dup_got,
    out_sem,
    out_got,
    gate_sem,
    gate_got,
    up_sem,
    up_got,
    spread_sem,
    spread_got,
):
    heads, _, rows = q_t.shape
    keys = latent.shape[0]
    tiles = keys // HALF
    last = contexts - 1
    half = two.shape[1]
    share = half // contexts
    d = lax.axis_index("dp")
    z = lax.axis_index("context")
    loads = [
        pltpu.make_async_copy(
            two_h.at[:, pl.ds(pl.multiple_of(d * half, 128), half)],
            two.at[0:rows],
            load_sem.at[0],
        ),
        pltpu.make_async_copy(far_two_h, two.at[rows : 2 * rows], load_sem.at[1]),
        pltpu.make_async_copy(dgate_h, act.at[0:rows], load_sem.at[2]),
        pltpu.make_async_copy(far_dgate_h, act.at[rows : 2 * rows], load_sem.at[3]),
    ]
    for load in loads:
        load.start()
    greet(line_of(z, contexts) + [{"dp": 1 - d}])

    swap_dup = pltpu.make_async_remote_copy(
        src_ref=dup_h,
        dst_ref=far_dup_o,
        send_sem=dup_sem,
        recv_sem=dup_got,
        device_id={"dp": 1 - d},
        device_id_type=MESH,
    )
    swap_dup.start()

    def line(src, dst, send_sem, recv_sem, way):
        return pltpu.make_async_remote_copy(
            src_ref=src,
            dst_ref=dst,
            send_sem=send_sem,
            recv_sem=recv_sem,
            device_id={"context": z + 1 - 2 * way},
            device_id_type=MESH,
        )

    along = [z, last - z]

    def spread(way, step):
        src = near_h.at[way] if step == 2 else spread_o.at[way, step - 3]
        i = (way, step - 2)
        return line(src, spread_o.at[i], spread_sem.at[i], spread_got.at[i], way)

    def spread_start(step):
        if step > last:
            return
        for way in range(2):
            if step > 2:

                @pl.when(along[way] >= step - 1)
                def _():
                    spread(way, step - 1).wait_recv()

            @pl.when((along[way] >= step - 1) & (along[way] < last))
            def _():
                spread(way, step).start()

    def spread_end():
        for way in range(2):
            for step in range(2, last + 1):
                if step == last:

                    @pl.when(along[way] >= step)
                    def _():
                        spread(way, step).wait_recv()

                @pl.when((along[way] >= step - 1) & (along[way] < last))
                def _():
                    spread(way, step).wait_send()

    def share_of(ref, index):
        return ref.at[pl.ds(pl.multiple_of(index * share, 16), share)]

    def farthest(way, step):
        right = z + 2 * contexts - step if way == 0 else contexts + step - 1 - along[1]
        return lax.rem(right, contexts)

    def reduce(ref, dst, send_sem, recv_sem, way, step):
        return line(
            share_of(ref, farthest(way, step)), dst, send_sem, recv_sem, way
        )

    def gate_step(way, step):
        i = (way, step - 1)
        return reduce(gate_w, arrived.at[i], gate_sem.at[i], gate_got.at[i], way, step)

    def up_step(way):
        return reduce(up_w, up_arrived.at[way], up_sem.at[way], up_got.at[way], way, 1)

    def add_rows(dst, src):
        @pl.loop(0, share // 16)
        def _(i):
            r = pl.ds(pl.multiple_of(i * 16, 16), 16)
            dst[r, :] = (dst[r, :].astype(F32) + src[r, :].astype(F32)).astype(BF16)

    def gate_start(step):
        if step > last:
            return
        for way in range(2):
            if step > 1:

                @pl.when((along[way] >= 1) & (along[way] < step))
                def _():
                    gate_step(way, step - 1).wait_recv()
                    add_rows(share_of(gate_w, farthest(way, step)), arrived.at[way, step - 2])

            @pl.when(along[way] < step)
            def _():
                gate_step(way, step).start()

    def gate_end():
        own = pl.multiple_of(z * share, 16)
        for way in range(2):

            @pl.when(along[way] >= 1)
            def _():
                gate_step(way, last).wait_recv()

        @pl.loop(0, share // 16)
        def _(i):
            r = pl.ds(pl.multiple_of(own + i * 16, 16), 16)
            q = pl.ds(pl.multiple_of(i * 16, 16), 16)
            value = gate_w[r, :].astype(F32)
            for way in range(2):
                value = jnp.where(
                    along[way] >= 1, value + arrived[way, last - 1, q, :].astype(F32), value
                )
            gate_o[q, :] = value

        for way in range(2):
            for step in range(1, last + 1):

                @pl.when(along[way] < step)
                def _():
                    gate_step(way, step).wait_send()

    upper = 1 - z // ((contexts + 1) // 2)
    count = half // 256

    def weight(ref, start):
        def tile(i):
            n = i + upper * (count - 1 - 2 * i)
            cols = pl.ds(pl.multiple_of(n * 256, 256), 256)
            ref[cols, :] = transposed_times(two[:, cols], act[...]).astype(BF16)

        pl.loop(0, 2)(tile)
        start()
        pl.loop(2, count)(tile)

    factor = SCALE * LOG2E
    row = lax.broadcasted_iota(jnp.int32, (HALF, rows), 0)
    spot = lax.broadcasted_iota(jnp.int32, (1, rows), 1)
    spot = jnp.where(
        spot < HALF, order[2 * z] * HALF + spot, order[2 * z + 1] * HALF + spot - HALF
    )

    def begin(g):
        for h in range(group):
            e = g * group + h
            span = slice(e * 128, (e + 1) * 128)
            kcat[h, :, :128] = matmul(latent[...], latent_up[:, span]).astype(BF16)
            kcat[h, :, 128:] = rope_keys[...]
            k_t[h, 0:64, :] = matmul(
                latent_up_t[e * 128 : e * 128 + 64, :], latent_t[...]
            ).astype(BF16)
            k_t[h, 64:96, :] = rope_keys_t[...]
            q_wide[h, 0:64, :] = q_t[e, 0:64, :]
            q_wide[h, 64:128, :] = jnp.zeros((64, rows), BF16)
            q_wide[h, 128:160, :] = q_t[e, 64:96, :]
            q_wide[h, 160:256, :] = jnp.zeros((96, rows), BF16)
            q_nat[h] = q_wide[h].T
            piece = dmix_t[e * V_DIM : (e + 1) * V_DIM, :]
            dmix_wide[h, 0:64, :] = jnp.zeros_like(piece)
            dmix_wide[h, 64:128, :] = piece
            dmix_nat[h] = dmix_wide[h].T
            delta[h] = jnp.sum(piece.astype(F32) * exact_t[e], axis=0, keepdims=True)
            dq[h] = jnp.zeros((96, rows), F32)

    def tiles_of(g, first, end):
        lane = lax.broadcasted_iota(jnp.int32, (1, 128), 1)
        scale = jnp.where(lane < NOPE, SCALE, 1.0).astype(F32)

        @pl.loop(first, end)
        def _(j):
            lines = pl.ds(pl.multiple_of(j * HALF, HALF), HALF)
            block = 2 * lax.rem(z + contexts - j // 2, contexts) + lax.rem(j, 2)
            allowed = row <= spot - order[block] * HALF
            turned = jnp.zeros((HALF, 128), F32)
            for h in range(group):
                e = g * group + h
                s = matmul(kcat[h, lines, :], q_wide[h])
                p = jnp.where(allowed, jnp.exp2(s * factor - lse[e]), 0.0)
                dp = matmul(kcat[h, lines, :128], dmix_wide[h])
                ds = (p * (dp - delta[h])).astype(BF16)
                dq[h] += matmul(k_t[h, :, lines], ds)
                dk = matmul(ds, q_nat[h])
                dv = matmul(p.astype(BF16), dmix_nat[h])
                pair[h, lines, :] = ((dk[:, :128] + dv) * scale).astype(BF16)
                turned += dk[:, 128:]
            rope_acc[lines, :] = turned if g == 0 else rope_acc[lines, :] + turned

    def finish(g):
        cosine = cos_t[...]
        sine = sin_t[...]
        for h in range(group):
            e = g * group + h
            span = slice(e * 128, (e + 1) * 128)
            value = dq[h] * SCALE
            first = value[64:80]
            second = value[80:96]
            dq_t[e, 0:64, :] = value[0:64].astype(BF16)
            dq_t[e, 64:80, :] = (first * cosine + second * sine).astype(BF16)
            dq_t[e, 80:96, :] = (second * cosine - first * sine).astype(BF16)
            grad_up[:, span] = matmul(latent_t[...], pair[h]).astype(BF16)
            change = times_transposed(latent_up[:, span], pair[h])
            lat_acc[...] = change if e == 0 else lat_acc[...] + change

    groups = heads // group
    total = groups * tiles
    stops = [total * (i + 1) // (last + 1) for i in range(last)]

    spread_start(2)
    for load in loads:
        load.wait()
    weight(gate_w, lambda: gate_start(1))
    done = 0
    for i, stop in enumerate(stops + [total]):
        while done < stop:
            g = done // tiles
            until = min(stop, (g + 1) * tiles)
            if done == g * tiles:
                begin(g)
            tiles_of(g, done - g * tiles, until - g * tiles)
            if until == (g + 1) * tiles:
                finish(g)
            done = until
        if i < last:
            gate_start(i + 2)
            spread_start(i + 3)
        if i == min(1, last - 1):
            swap_dup.wait_recv()
            again = [
                pltpu.make_async_copy(dup_h, act.at[0:rows], load_sem.at[2]),
                pltpu.make_async_copy(far_dup_o, act.at[rows : 2 * rows], load_sem.at[3]),
            ]
            for load in again:
                load.start()
            for load in again:
                load.wait()

            def up_start():
                for way in range(2):

                    @pl.when(along[way] == 0)
                    def _():
                        up_step(way).start()

            weight(up_w, up_start)
            parts = [
                pltpu.make_async_copy(
                    dbranch_h.at[:, e * half : (e + 1) * half],
                    two.at[e * rows : (e + 1) * rows],
                    load_sem.at[2 + e],
                )
                for e in range(2)
            ]
            for load in parts:
                load.start()
            keep = pltpu.make_async_copy(up_w, up_o, load_sem.at[0])
            keep.start()
            joined[...] = joined_t[...].T
            for load in parts:
                load.wait()
            for e in range(2):

                @pl.loop(0, half // 256)
                def _(n):
                    cols = pl.ds(pl.multiple_of(n * 256, 256), 256)
                    lines = pl.ds(pl.multiple_of(e * half + n * 256, 256), 256)
                    out_w[lines, :] = transposed_times(
                        two[e * rows : (e + 1) * rows, cols], joined[...]
                    ).astype(BF16)

            swap_out = pltpu.make_async_remote_copy(
                src_ref=out_w.at[pl.ds(pl.multiple_of((1 - d) * half, 16), half)],
                dst_ref=far_out_o,
                send_sem=out_sem,
                recv_sem=out_got,
                device_id={"dp": 1 - d},
                device_id_type=MESH,
            )
            swap_out.start()
            keep_out = pltpu.make_async_copy(
                out_w.at[pl.ds(pl.multiple_of(d * half, 16), half)], out_o, load_sem.at[1]
            )
            keep_out.start()

    dlat_t[0:KV_RANK, :] = lat_acc[...].astype(BF16)
    dlat_t[KV_RANK:, :] = (rope_acc[...] * SCALE).T[:ROPE].astype(BF16)
    gate_end()
    spread_end()
    keep.wait()
    keep_out.wait()
    swap_dup.wait_send()
    for way in range(2):

        @pl.when(along[way] == 0)
        def _():
            up_step(way).wait_send()

        @pl.when(along[way] == 1)
        def _():
            up_step(way).wait_recv()
            piece = share_of(up_w, farthest(way, 2))
            add_rows(piece, up_arrived.at[way])
            again = pltpu.make_async_copy(
                piece, share_of(up_o, farthest(way, 2)), load_sem.at[2]
            )
            again.start()
            again.wait()

    swap_out.wait()


def backward(
    contexts,
    order,
    q_t,
    latent,
    latent_t,
    rope_keys,
    rope_keys_t,
    latent_up,
    latent_up_t,
    exact_t,
    lse,
    dmix_t,
    cos_t,
    sin_t,
    joined_t,
    two,
    far_two,
    dgate,
    far_dgate,
    dup,
    near,
    dbranch,
):
    heads, _, rows = q_t.shape
    keys = latent.shape[0]
    group = GROUP
    units = dup.shape[1]
    half = far_two.shape[1]
    share = half // contexts
    last = contexts - 1
    anywhere = pl.BlockSpec(memory_space=pl.ANY)
    inside = pl.BlockSpec(memory_space=pltpu.VMEM)
    dma = pltpu.SemaphoreType.DMA
    return pl.pallas_call(
        functools.partial(backward_kernel, contexts, group),
        in_specs=[pl.BlockSpec(memory_space=pltpu.SMEM)] + [inside] * 13 + [anywhere] * 7,
        out_specs=[inside] * 4 + [anywhere] * 5,
        out_shape=[
            jax.ShapeDtypeStruct((heads, 96, rows), BF16),
            jax.ShapeDtypeStruct((KV_RANK, heads * 128), BF16),
            jax.ShapeDtypeStruct((KV_RANK + ROPE, keys), BF16),
            jax.ShapeDtypeStruct((share, units), F32),
            jax.ShapeDtypeStruct((half, units), BF16),
            jax.ShapeDtypeStruct((half, joined_t.shape[0]), BF16),
            jax.ShapeDtypeStruct((half, joined_t.shape[0]), BF16),
            jax.ShapeDtypeStruct((rows, units), BF16),
            jax.ShapeDtypeStruct((2, last - 1, rows, units), BF16),
        ],
        scratch_shapes=[
            pltpu.VMEM((group, keys, 256), BF16),
            pltpu.VMEM((group, 96, keys), BF16),
            pltpu.VMEM((group, 256, rows), BF16),
            pltpu.VMEM((group, 128, rows), BF16),
            pltpu.VMEM((group, rows, 256), BF16),
            pltpu.VMEM((group, rows, 128), BF16),
            pltpu.VMEM((group, 1, rows), F32),
            pltpu.VMEM((group, 96, rows), F32),
            pltpu.VMEM((group, keys, 128), BF16),
            pltpu.VMEM((KV_RANK, keys), F32),
            pltpu.VMEM((keys, 128), F32),
            pltpu.VMEM((2 * rows, half), BF16),
            pltpu.VMEM((2 * rows, units), BF16),
            pltpu.VMEM((half, units), BF16),
            pltpu.VMEM((half, units), BF16),
            pltpu.VMEM((2, last, share, units), BF16),
            pltpu.VMEM((2, share, units), BF16),
            pltpu.VMEM((2 * half, joined_t.shape[0]), BF16),
            pltpu.VMEM((rows, joined_t.shape[0]), BF16),
            dma((4,)),
            dma,
            dma,
            dma,
            dma,
            dma((2, last)),
            dma((2, last)),
            dma((2,)),
            dma((2,)),
            dma((2, last - 1)),
            dma((2, last - 1)),
        ],
        compiler_params=pltpu.CompilerParams(
            collective_id=1, has_side_effects=True, vmem_limit_bytes=65000 * 1024
        ),
        cost_estimate=pl.CostEstimate(
            flops=2 * heads * rows * keys * 1000,
            bytes_accessed=40 * 1024 * 1024,
            transcendentals=heads * rows * keys,
        ),
        name="backward",
    )(
        order,
        q_t,
        latent,
        latent_t,
        rope_keys,
        rope_keys_t,
        latent_up,
        latent_up_t,
        exact_t,
        lse,
        dmix_t,
        cos_t,
        sin_t,
        joined_t,
        two,
        far_two,
        dgate,
        far_dgate,
        dup,
        near,
        dbranch,
    )


def tail_kernel(
    contexts,
    tensors,
    split,
    dq_t,
    query_up_t,
    query_t,
    query_normed,
    query_inverse,
    all_gains,
    dlat,
    cache_t,
    cache_inverse_t,
    cos_t,
    sin_t,
    lat_grad,
    first_inverse,
    mlp_gain_grad,
    out_h,
    far_out_h,
    hidden_h,
    near_h,
    spread_h,
    feed_t_h,
    up_h,
    one_t_h,
    query_down_h,
    latent_down_t_h,
    tokens_h,
    feed_h,
    norm_o,
    low_q_o,
    low_l_o,
    small_q_o,
    small_l_o,
    out_o,
    up_o,
    down_o,
    gain_o,
    feed_o,
    q_part,
    q_near,
    q_across,
    q_final,
    d_near,
    d_acc,
    d_across,
    d_got,
    d_all,
    d_final,
    u_w,
    u_far,
    u_got,
    l_far,
    l_got,
    wide,
    up_got,
    out_w,
    out_far,
    out_got,
    long,
    feed_t,
    down_w,
    down_far,
    f_part,
    f_near,
    f_across,
    dqa,
    dkva_t,
    one_t,
    low_q,
    low_l,
    low_q_far,
    low_l_far,
    low_q_got,
    low_l_got,
    low_q_all,
    low_l_all,
    query_down,
    latent_down_t,
    dh1,
    stage,
    gains,
    gains_far,
    gains_got,
    send_sem,
    recv_sem,
    load_sem,
):
    rows = dlat.shape[1] // contexts
    width = wide.shape[1]
    half = width // 2
    share = half // contexts
    last = contexts - 1
    rank = query_normed.shape[1]
    kv = cache_t.shape[0]
    first_gain = slice(0, width)
    query_gain = slice(2 * width, 2 * width + rank)
    latent_gain = slice(2 * width + rank, 2 * width + rank + kv)
    d = lax.axis_index("dp")
    z = lax.axis_index("context")
    t = lax.axis_index("tensor")
    bit = lax.rem(t, 2)
    others = [t + 1 - 2 * bit]
    step = 2
    while step < tensors:
        others.append(t + step - 2 * step * lax.rem(t // step, 2))
        step *= 2
    spot = lax.rem(t, split)
    sharers = [t - spot + lax.rem(spot + k, split) for k in range(1, split)]

    used = [0]

    def remote(src, dst, **device):
        i = used[0]
        used[0] += 1
        return pltpu.make_async_remote_copy(
            src_ref=src,
            dst_ref=dst,
            send_sem=send_sem.at[i],
            recv_sem=recv_sem.at[i],
            device_id=device,
            device_id_type=MESH,
        )

    loaded = [0]

    def local(src, dst):
        i = loaded[0]
        loaded[0] += 1
        return pltpu.make_async_copy(src, dst, load_sem.at[i])

    def only(condition, copy, what):
        @pl.when(condition)
        def _():
            getattr(copy, what)()

    def add_rows(dst, left, right, count, chunk=16):
        @pl.loop(0, count // chunk)
        def _(i):
            r = pl.ds(pl.multiple_of(i * chunk, chunk), chunk)
            dst[r, :] = (left[r, :].astype(F32) + right[r, :].astype(F32)).astype(BF16)

    def piece(ref, index, size):
        return ref.at[pl.ds(pl.multiple_of(index * size, 16), size)]

    load_out = [local(out_h, out_w), local(far_out_h, out_far)]
    load_tokens = local(tokens_h, wide)
    load_hidden = [(None, local(hidden_h, long.at[0:rows]))]
    for s in range(1, contexts):
        back = contexts - s
        dst = long.at[s * rows : (s + 1) * rows]
        right = near_h.at[0] if s == 1 else spread_h.at[0, s - 2]
        left = near_h.at[1] if back == 1 else spread_h.at[1, back - 2]
        load_hidden.append((z >= s, local(right, dst)))
        load_hidden.append((z < s, local(left, dst)))
    load_feed_t = local(feed_t_h, feed_t)
    load_one = local(one_t_h, one_t)
    load_down = [local(query_down_h, query_down), local(latent_down_t_h, latent_down_t)]

    def load_feed(c):
        return [
            local(
                feed_h.at[pl.ds(c * CHUNK, CHUNK), h * half : (h + 1) * half], f_part.at[h]
            )
            for h in range(2)
        ]

    feed_loads = [load_feed(c) for c in range(rows // CHUNK)]
    for copy in load_out:
        copy.start()
    load_feed_t.start()
    for condition, copy in load_hidden:
        if condition is None:
            copy.start()
        else:
            only(condition, copy, "start")
    for copy in [load_one, load_tokens] + load_down + feed_loads[0]:
        copy.start()

    peers = others if split == 2 else sharers
    greet([{"tensor": i} for i in peers] + line_of(z, contexts) + [{"dp": 1 - d}])

    along = [z, last - z]

    def farthest(way, step):
        right = z + 2 * contexts - step if way == 0 else contexts + step - 1 - along[1]
        return lax.rem(right, contexts)

    def line_step(w, got, way, step, first):
        return remote(
            piece(w, farthest(way, step), share),
            got.at[way, step - first],
            context=z + 1 - 2 * way,
        )

    up_w = long
    up_steps = {
        (way, step): line_step(up_h if step == 2 else up_w, up_got, way, step, 2)
        for way in range(2)
        for step in range(2, last + 1)
    }
    out_steps = {
        (way, step): line_step(out_far, out_got, way, step, 1)
        for way in range(2)
        for step in range(1, last + 1)
    }

    def line_start(steps, w, got, first, step):
        for way in range(2):
            if step > first:

                @pl.when((along[way] >= 1) & (along[way] < step))
                def _():
                    steps[way, step - 1].wait_recv()
                    target = piece(w, farthest(way, step), share)
                    add_rows(target, target, got.at[way, step - 1 - first], share)

            only(along[way] < step, steps[way, step], "start")

    def line_end(steps, w, got, first, result):
        for way in range(2):
            only(along[way] >= 1, steps[way, last], "wait_recv")

        @pl.loop(0, share // 16)
        def _(i):
            r = pl.ds(pl.multiple_of(z * share + i * 16, 16), 16)
            q = pl.ds(pl.multiple_of(i * 16, 16), 16)
            value = w[r, :].astype(F32)
            for way in range(2):
                value = jnp.where(
                    along[way] >= 1, value + got[way, last - first, q, :].astype(F32), value
                )
            result[q, :] = value

        for way in range(2):
            for step in range(first, last + 1):
                only(along[way] < step, steps[way, step], "wait_send")

    line_start(up_steps, up_w, up_got, 2, 2)

    d_rows = dlat.shape[0] // 2
    d_pair = remote(dlat.at[pl.ds(pl.multiple_of((1 - bit) * d_rows, 16), d_rows)], d_near, tensor=others[0])
    d_pair.start()

    q_rows = rows // 2
    for h in range(2):
        q_part[h] = transposed_times(
            dq_t[:, h * q_rows : (h + 1) * q_rows], query_up_t[...]
        ).astype(BF16)
    q_pair = remote(q_part.at[1 - bit], q_near, tensor=others[0])
    q_pair.start()

    for copy in load_out:
        copy.wait()
    add_rows(out_far, out_far, out_w, half, 32)
    line_start(out_steps, out_far, out_got, 1, 1)

    u_w[...] = times_transposed(query_t[...], dq_t[...]).astype(BF16)
    u_half = u_w.shape[0] // 2
    l_half = lat_grad.shape[0] // 2
    u_pair = remote(
        u_w.at[pl.ds(pl.multiple_of((1 - d) * u_half, 16), u_half)], u_far, dp=1 - d
    )
    l_pair = remote(
        lat_grad.at[pl.ds(pl.multiple_of((1 - d) * l_half, 16), l_half)], l_far, dp=1 - d
    )
    u_pair.start()
    l_pair.start()

    d_pair.wait_recv()
    mine = pl.multiple_of(bit * d_rows, 16)

    @pl.loop(0, d_rows // 16)
    def _(i):
        r = pl.ds(pl.multiple_of(i * 16, 16), 16)
        own = pl.ds(pl.multiple_of(mine + i * 16, 16), 16)
        value = (dlat[own, :].astype(F32) + d_near[r, :].astype(F32)).astype(BF16)
        for s in range(contexts):
            d_acc[s, r, :] = value[:, s * rows : (s + 1) * rows]

    d_hops = []
    lanes = rows
    start = 0
    for k in range(1, len(others)):
        lanes //= 2
        side = lax.rem(t // (2**k), 2)
        give = pl.ds(pl.multiple_of(start + (1 - side) * lanes, 128), lanes)
        start = pl.multiple_of(start + side * lanes, 128)
        d_hops.append(
            (remote(d_acc.at[:, :, give], d_across.at[k - 1, :, :, 0:lanes], tensor=others[k]),
             start, lanes)
        )

    d_hops[0][0].start()
    q_pair.wait_recv()
    add_rows(q_near, q_near, q_part.at[bit], q_rows, 32)
    q_hops = []
    for k in range(1, len(others)):
        src = q_near if k == 1 else q_across.at[k - 2]
        q_hops.append(remote(src, q_across.at[k - 1], tensor=others[k]))
    q_hops[0].start()

    load_feed_t.wait()
    for condition, copy in load_hidden:
        if condition is None:
            copy.wait()
        else:
            only(condition, copy, "wait")
    chunk = 2 * share // 5 if (2 * share // 5) % 16 == 0 else share

    @pl.loop(0, 2 * share // chunk)
    def _(i):
        r = pl.ds(pl.multiple_of(i * chunk, 16), chunk)
        down_w[r, :] = matmul(feed_t[r, :], long[...]).astype(BF16)

    load_up = local(up_h, long.at[0:half])
    load_up.start()
    down_pair = remote(piece(down_w, 1 - d, share), down_far, dp=1 - d)

    f_pairs, f_hops, f_backs = [], [], []
    for c in range(rows // CHUNK):
        span = pl.ds(c * CHUNK, CHUNK)
        f_pairs.append(remote(f_part.at[1 - bit], f_near.at[c], tensor=others[0]))
        hops = []
        for k in range(1, len(others)):
            src = f_near.at[c] if k == 1 else f_across.at[k - 2, c]
            hops.append(remote(src, f_across.at[k - 1, c], tensor=others[k]))
        f_hops.append(hops)
        here = f_across.at[len(others) - 2, c]
        f_backs.append(
            (remote(here, feed_o.at[span, pl.ds(pl.multiple_of(bit * half, 128), half)], tensor=others[0]), local(here, feed_o.at[span, pl.ds(pl.multiple_of(bit * half, 128), half)]))
        )

    def feed_pair(c):
        for copy in feed_loads[c]:
            copy.wait()
        f_pairs[c].start()

    def feed_across(c):
        f_pairs[c].wait_recv()
        add_rows(f_near.at[c], f_near.at[c], f_part.at[bit], CHUNK, 32)
        f_hops[c][0].start()
        f_pairs[c].wait_send()
        if c + 1 < rows // CHUNK:
            for copy in feed_loads[c + 1]:
                copy.start()

    def feed_back(c):
        for k, hop in enumerate(f_hops[c]):
            hop.wait_recv()
            src = f_near.at[c] if k == 0 else f_across.at[k - 1, c]
            add_rows(f_across.at[k, c], src, f_across.at[k, c], CHUNK, 32)
            if k < len(f_hops[c]) - 1:
                f_hops[c][k + 1].start()
        for back in f_backs[c]:
            back.start()


    for k, (hop, begin, lane) in enumerate(d_hops):
        hop.wait_recv()
        keep = pl.ds(begin, lane)

        @pl.loop(0, contexts)
        def _(s):
            @pl.loop(0, d_rows // 16)
            def _(i):
                r = pl.ds(pl.multiple_of(i * 16, 16), 16)
                d_acc[s, r, keep] = (
                    d_acc[s, r, keep].astype(F32) + d_across[k, s, r, 0:lane].astype(F32)
                ).astype(BF16)

        if k + 1 < len(d_hops):
            d_hops[k + 1][0].start()
    keep = pl.ds(start, lanes)
    d_sends = [
        remote(
            d_acc.at[s, :, keep],
            d_got.at[s - 1],
            context=lax.rem(z + contexts - s, contexts),
        )
        for s in range(1, contexts)
    ]
    for copy in d_sends:
        copy.start()
    final = len(q_hops) - 1
    for k, hop in enumerate(q_hops):
        hop.wait_recv()
        src = q_near if k == 0 else q_across.at[k - 1]
        dst = q_final.at[bit] if k == final else q_across.at[k]
        add_rows(dst, src, q_across.at[k], q_rows, 32)
        if k < final:
            q_hops[k + 1].start()
    q_back = remote(q_final.at[bit], q_final.at[bit], tensor=others[0])
    q_back.start()

    feed_pair(0)
    line_start(out_steps, out_far, out_got, 1, 2) if last >= 2 else None
    load_up.wait()
    line_start(up_steps, up_w, up_got, 2, 3) if last >= 3 else None
    u_pair.wait_recv()
    l_pair.wait_recv()

    @pl.loop(0, u_half // 16)
    def _(i):
        r = pl.ds(pl.multiple_of(i * 16, 16), 16)
        own = pl.ds(pl.multiple_of(d * u_half + i * 16, 16), 16)
        u_far[r, :] = (u_far[r, :].astype(F32) + u_w[own, :].astype(F32)).astype(BF16)

    @pl.loop(0, l_half // 16)
    def _(i):
        r = pl.ds(pl.multiple_of(i * 16, 16), 16)
        own = pl.ds(pl.multiple_of(d * l_half + i * 16, 16), 16)
        l_far[r, :] = (l_far[r, :].astype(F32) + lat_grad[own, :].astype(F32)).astype(BF16)

    u_size = u_half // contexts
    l_size = l_half // contexts
    small_sends = []
    for by in range(1, contexts):
        owner = lax.rem(z + by, contexts)
        small_sends.append(remote(piece(u_far, owner, u_size), u_got.at[by - 1], context=owner))
        small_sends.append(remote(piece(l_far, owner, l_size), l_got.at[by - 1], context=owner))
    for copy in small_sends:
        copy.start()
    feed_across(0)

    q_back.wait_recv()
    q_sum = jnp.zeros((8, rank), F32)

    def query_rows(i, acc):
        r = pl.ds(pl.multiple_of(i * 32, 32), 32)
        h = i // (q_rows // 32)
        o = pl.ds(pl.multiple_of(lax.rem(i, q_rows // 32) * 32, 32), 32)
        grad = q_final[h, o, :].astype(F32)
        normed = query_normed[r, :].astype(F32)
        weighted = grad * all_gains[:, query_gain]
        mean = jnp.mean(weighted * normed, axis=-1, keepdims=True)
        dqa[r, :] = (query_inverse[r, :] * (weighted - normed * mean)).astype(BF16)
        return acc + jnp.sum((grad * normed).reshape(4, 8, rank), axis=0)

    q_sum = lax.fori_loop(0, rows // 32, query_rows, q_sum)

    for copy in d_sends:
        copy.wait_recv()

    @pl.loop(0, d_rows // 16)
    def _(i):
        r = pl.ds(pl.multiple_of(i * 16, 16), 16)
        value = d_acc[0, r, keep].astype(F32)
        for s in range(1, contexts):
            value += d_got[s - 1, r, :].astype(F32)
        d_all[r, keep] = value.astype(BF16)

    d_gathers = []
    for k in range(len(others) - 1, 0, -1):
        here = d_all.at[:, pl.ds(start, lanes)]
        hop = remote(here, here, tensor=others[k])
        hop.start()
        hop.wait_recv()
        d_gathers.append(hop)
        side = lax.rem(t // (2**k), 2)
        start = pl.multiple_of(start - side * lanes, 128)
        lanes *= 2
    d_back = remote(d_all, d_final, tensor=others[0])
    d_back.start()
    if rows // CHUNK > 1:
        feed_pair(1)
    d_back.wait_recv()

    top = jnp.where(bit == 0, d_all[...], d_final[...]).astype(F32)
    bottom = jnp.where(bit == 0, d_final[...], d_all[...]).astype(F32)
    grad = jnp.concatenate([top, bottom], axis=0)
    lat = grad[:kv]
    normed = cache_t[...].astype(F32)
    column = jnp.broadcast_to(all_gains[:, latent_gain], (8, kv)).T[:, 0:1]
    weighted = lat * column
    mean = jnp.mean(weighted * normed, axis=0, keepdims=True)
    dkva_t[0:kv, :] = (cache_inverse_t[...] * (weighted - normed * mean)).astype(BF16)
    c_sum = jnp.sum((lat * normed).T, axis=0, keepdims=True)
    first = grad[kv : kv + 16]
    second = grad[kv + 16 :]
    cosine = cos_t[...]
    sine = sin_t[...]
    dkva_t[kv : kv + 16, :] = (first * cosine + second * sine).astype(BF16)
    dkva_t[kv + 16 :, :] = (second * cosine - first * sine).astype(BF16)

    load_one.wait()
    size = share // split

    @pl.loop(0, 2 * contexts)
    def _(i):
        r = pl.ds(pl.multiple_of((i * split + spot) * size, 16), size)
        o = pl.ds(pl.multiple_of(i * size, 16), size)
        low_q[o, :] = matmul(one_t[r, :], dqa[...]).astype(BF16)
        low_l[o, :] = times_transposed(one_t[r, :], dkva_t[...]).astype(BF16)

    low_half = contexts * size
    give = pl.ds(pl.multiple_of((1 - d) * low_half, 16), low_half)
    low_pairs = [
        remote(low_q.at[give], low_q_far, dp=1 - d),
        remote(low_l.at[give], low_l_far, dp=1 - d),
    ]
    for copy in low_pairs:
        copy.start()
    down_pair.start()
    line_start(out_steps, out_far, out_got, 1, 3) if last >= 3 else None
    if rows // CHUNK > 1:
        feed_across(1)

    for copy in load_down:
        copy.wait()
    load_tokens.wait()
    a_sum = jnp.zeros((8, width), F32)
    gains[...] = jnp.zeros_like(gains)
    block = dh1.shape[0]
    tall = 512

    def first_rows(c, acc):
        span = pl.ds(pl.multiple_of(c * block, block), block)
        for n in range(width // tall):
            lines = slice(n * tall, (n + 1) * tall)
            dh1[:, lines] = times_transposed(dqa[span, :], query_down[lines, :])
            dh1[:, lines] += transposed_times(dkva_t[:, span], latent_down_t[:, lines])

        def few(i, inner):
            o = pl.ds(pl.multiple_of(i * 16, 16), 16)
            r = pl.ds(pl.multiple_of(c * block + i * 16, 16), 16)
            grad = dh1[o, :]
            inverse = first_inverse[r, :]
            normed = wide[r, :].astype(F32) * inverse
            weighted = grad * all_gains[:, first_gain]
            mean = jnp.mean(weighted * normed, axis=-1, keepdims=True)
            wide[r, :] = (inverse * (weighted - normed * mean)).astype(BF16)
            return inner + jnp.sum((grad * normed).reshape(2, 8, width), axis=0)

        return lax.fori_loop(0, block // 16, few, acc)

    for c in range(rows // block):
        a_sum = first_rows(c, a_sum)
    save_norm = local(wide, norm_o)
    save_norm.start()

    parts = [
        jnp.sum(a_sum, axis=0, keepdims=True),
        jnp.sum(mlp_gain_grad[...], axis=0, keepdims=True),
        jnp.sum(q_sum, axis=0, keepdims=True),
        c_sum,
    ]
    line = jnp.concatenate(parts, axis=1)
    cut = gains.shape[1]
    for r in range(8):
        gains[r : r + 1, :] = line[:, r * cut : (r + 1) * cut]
    gains_pair = remote(gains, gains_far, dp=1 - d)
    gains_pair.start()

    feed_back(0)
    gains_pair.wait_recv()
    gains_far[...] = gains_far[...] + gains[...]
    gains_sends = [
        remote(gains_far, gains_got.at[by - 1], context=lax.rem(z + by, contexts))
        for by in range(1, contexts)
    ]
    for copy in gains_sends:
        copy.start()
    for copy in low_pairs:
        copy.wait_recv()

    @pl.loop(0, low_half // 16)
    def _(i):
        r = pl.ds(pl.multiple_of(i * 16, 16), 16)
        own = pl.ds(pl.multiple_of(d * low_half + i * 16, 16), 16)
        low_q_far[r, :] = (
            low_q_far[r, :].astype(F32) + low_q[own, :].astype(F32)
        ).astype(BF16)
        low_l_far[r, :] = (
            low_l_far[r, :].astype(F32) + low_l[own, :].astype(F32)
        ).astype(BF16)

    low_sends = []
    for by in range(1, contexts):
        owner = lax.rem(z + by, contexts)
        low_sends.append(
            remote(piece(low_q_far, owner, size), low_q_got.at[by - 1], context=owner)
        )
        low_sends.append(
            remote(piece(low_l_far, owner, size), low_l_got.at[by - 1], context=owner)
        )
    for copy in low_sends:
        copy.start()
    for copy in small_sends:
        copy.wait_recv()
    for far, got, result, count in (
        (u_far, u_got, small_q_o, u_size),
        (l_far, l_got, small_l_o, l_size),
    ):

        @pl.loop(0, count // 16)
        def _(i):
            r = pl.ds(pl.multiple_of(z * count + i * 16, 16), 16)
            q = pl.ds(pl.multiple_of(i * 16, 16), 16)
            value = far[r, :].astype(F32)
            for by in range(1, contexts):
                value += got[by - 1, q, :].astype(F32)
            result[q, :] = value

    for step in range(4, last + 1):
        line_start(out_steps, out_far, out_got, 1, step)
        line_start(up_steps, up_w, up_got, 2, step)
    if rows // CHUNK > 1:
        feed_back(1)
    for copy in low_sends:
        copy.wait_recv()

    @pl.loop(0, size // 16)
    def _(i):
        r = pl.ds(pl.multiple_of(z * size + i * 16, 16), 16)
        q = pl.ds(pl.multiple_of(i * 16, 16), 16)
        for far, got, everyone in (
            (low_q_far, low_q_got, low_q_all),
            (low_l_far, low_l_got, low_l_all),
        ):
            value = far[r, :].astype(F32)
            for by in range(1, contexts):
                value += got[by - 1, q, :].astype(F32)
            everyone[spot, q, :] = value.astype(BF16)

    low_gathers = []
    for sharer in sharers:
        for everyone in (low_q_all, low_l_all):
            here = everyone.at[spot]
            copy = remote(here, here, tensor=sharer)
            copy.start()
            low_gathers.append(copy)
    down_pair.wait_recv()

    @pl.loop(0, share // 16)
    def _(i):
        r = pl.ds(pl.multiple_of(d * share + i * 16, 16), 16)
        q = pl.ds(pl.multiple_of(i * 16, 16), 16)
        stage[q, :] = down_w[r, :].astype(F32) + down_far[q, :].astype(F32)

    save_down = local(stage, down_o)
    save_down.start()
    save_down.wait()

    line_end(up_steps, up_w, up_got, 2, stage)
    save_up = local(stage, up_o)
    save_up.start()
    for copy in gains_sends:
        copy.wait_recv()
    value = gains_far[...]
    for by in range(1, contexts):
        value += gains_got[by - 1]
    gain_o[...] = value
    for copy in low_gathers:
        copy.wait_recv()
    save_low = [local(low_q_all, low_q_o), local(low_l_all, low_l_o)]
    for copy in save_low:
        copy.start()
    line_end(out_steps, out_far, out_got, 1, out_o)
    for copy in save_low + [save_norm, save_up]:
        copy.wait()
    for back, save in f_backs:
        back.wait_recv()
        save.wait()
    sent = [d_pair, q_pair, u_pair, l_pair, q_back, d_back, down_pair, gains_pair]
    sent += q_hops + [hop[0] for hop in d_hops] + d_sends + d_gathers + small_sends
    sent += low_pairs + low_sends + low_gathers + gains_sends + [back[0] for back in f_backs]
    for hops in f_hops:
        sent += hops
    for copy in sent:
        copy.wait_send()


def tail(contexts, tensors, split, inside_args, outside_args):
    dq_t, query_t, dlat, lat_grad = (inside_args[i] for i in (0, 2, 6, 11))
    out_cols = outside_args[0].shape[1]
    rows = query_t.shape[1]
    rank = query_t.shape[0]
    width = outside_args[9].shape[1]
    units = outside_args[2].shape[1]
    half = width // 2
    share = half // contexts
    size = share // split
    last = contexts - 1
    hops = tensors.bit_length() - 1
    kv = dlat.shape[0]
    d_rows = kv // 2
    lanes = rows >> (hops - 1)
    heads_q = dq_t.shape[0]
    lat_rows, lat_cols = lat_grad.shape
    count_gains = (2 * width + rank + lat_rows) // 8
    anywhere = pl.BlockSpec(memory_space=pl.ANY)
    inside = pl.BlockSpec(memory_space=pltpu.VMEM)
    vm = pltpu.VMEM
    sds = jax.ShapeDtypeStruct
    chunks = rows // CHUNK
    return pl.pallas_call(
        functools.partial(tail_kernel, contexts, tensors, split),
        in_specs=[inside] * len(inside_args) + [anywhere] * len(outside_args),
        out_specs=[anywhere] * 3 + [inside] * 3 + [anywhere] * 2 + [inside, anywhere],
        out_shape=[
            sds((rows, width), BF16),
            sds((split, size, rank), BF16),
            sds((split, size, kv), BF16),
            sds((rank // (2 * contexts), heads_q), F32),
            sds((lat_rows // (2 * contexts), lat_cols), F32),
            sds((share, out_cols), F32),
            sds((share, units), F32),
            sds((share, units), F32),
            sds((8, count_gains), F32),
            sds((rows, width), BF16),
        ],
        scratch_shapes=[
            vm((2, rows // 2, rank), BF16),
            vm((rows // 2, rank), BF16),
            vm((hops - 1, rows // 2, rank), BF16),
            vm((2, rows // 2, rank), BF16),
            vm((d_rows, contexts * rows), BF16),
            vm((contexts, d_rows, rows), BF16),
            vm((hops - 1, contexts, d_rows, rows // 2), BF16),
            vm((last, d_rows, lanes), BF16),
            vm((d_rows, rows), BF16),
            vm((d_rows, rows), BF16),
            vm((rank, heads_q), BF16),
            vm((rank // 2, heads_q), BF16),
            vm((last, rank // (2 * contexts), heads_q), BF16),
            vm((lat_rows // 2, lat_cols), BF16),
            vm((last, lat_rows // (2 * contexts), lat_cols), BF16),
            vm((rows, width), BF16),
            vm((2, last - 1, share, units), BF16),
            vm((half, out_cols), BF16),
            vm((half, out_cols), BF16),
            vm((2, last, share, out_cols), BF16),
            vm((contexts * rows, units), BF16),
            vm((2 * share, contexts * rows), BF16),
            vm((2 * share, units), BF16),
            vm((share, units), BF16),
            vm((2, CHUNK, half), BF16),
            vm((chunks, CHUNK, half), BF16),
            vm((hops - 1, chunks, CHUNK, half), BF16),
            vm((rows, rank), BF16),
            vm((kv, rows), BF16),
            vm((width, rows), BF16),
            vm((2 * contexts * size, rank), BF16),
            vm((2 * contexts * size, kv), BF16),
            vm((contexts * size, rank), BF16),
            vm((contexts * size, kv), BF16),
            vm((last, size, rank), BF16),
            vm((last, size, kv), BF16),
            vm((split, size, rank), BF16),
            vm((split, size, kv), BF16),
            vm((width, rank), BF16),
            vm((kv, width), BF16),
            vm((128, width), F32),
            vm((share, units), F32),
            vm((8, count_gains), F32),
            vm((8, count_gains), F32),
            vm((last, 8, count_gains), F32),
            pltpu.SemaphoreType.DMA((128,)),
            pltpu.SemaphoreType.DMA((128,)),
            pltpu.SemaphoreType.DMA((48,)),
        ],
        compiler_params=pltpu.CompilerParams(
            collective_id=2, has_side_effects=True, vmem_limit_bytes=65000 * 1024
        ),
        cost_estimate=pl.CostEstimate(
            flops=2 * rows * width * units * 3, bytes_accessed=40 * 1024 * 1024, transcendentals=0
        ),
        name="tail",
    )(*inside_args, *outside_args)


def finish_kernel(
    count,
    tokens,
    branch,
    feed,
    dmiddle,
    norm_one,
    low_q,
    low_l,
    *rest,
):
    given = rest[:count]
    layer_out, token_grad, low_q_o, low_l_o = rest[count : count + 4]
    taken = rest[count + 4 :]
    for src, dst in zip(given, taken):
        dst[...] = src[...]

    @pl.when(pl.program_id(0) == 0)
    def _():
        low_q_o[...] = low_q[...].astype(F32)
        low_l_o[...] = low_l[...].astype(F32).T

    added = branch[...].astype(F32) + feed[...].astype(F32)
    layer_out[...] = (tokens[...].astype(F32) + RESIDUAL * added).astype(BF16)
    token_grad[...] = dmiddle[...] + norm_one[...].astype(F32)


def finish(tokens, branch, feed, dmiddle, norm_one, low_q, low_l, given):
    rows, width = tokens.shape
    steps = 4
    tiled = pl.BlockSpec((rows // steps, width), lambda i: (i, 0))
    passed = [
        pl.BlockSpec((g.shape[0] // steps, g.shape[1]), lambda i: (i, 0))
        if g.shape[0] % (8 * steps) == 0
        else whole_spec(g.shape)
        for g in given
    ]
    sds = jax.ShapeDtypeStruct
    return pl.pallas_call(
        functools.partial(finish_kernel, len(given)),
        grid=(steps,),
        in_specs=[tiled] * 5
        + [whole_spec(low_q.shape), whole_spec(low_l.shape)]
        + passed,
        out_specs=[tiled] * 2
        + [whole_spec(low_q.shape), whole_spec(low_l.shape[::-1])]
        + passed,
        out_shape=[
            sds((rows, width), BF16),
            sds((rows, width), F32),
            sds(low_q.shape, F32),
            sds(low_l.shape[::-1], F32),
        ]
        + [sds(g.shape, g.dtype) for g in given],
        compiler_params=pltpu.CompilerParams(vmem_limit_bytes=65000 * 1024),
        name="finish",
    )(tokens, branch, feed, dmiddle, norm_one, low_q, low_l, *given)


def pick(value, index):
    return lax.dynamic_index_in_dim(value, index, 0, keepdims=False)


def per_device(
    sizes,
    tokens,
    cotangent,
    group_order,
    attn_gain,
    query_down,
    query_gain,
    latent_down,
    latent_gain,
    query_up,
    latent_up,
    attn_out,
    mlp_gain,
    gate_proj,
    up_proj,
    down_proj,
):
    contexts, tensors = sizes
    rows, width = tokens.shape[1:]
    heads = query_up.shape[1] // (NOPE + ROPE)
    z = lax.axis_index("context")
    d = lax.axis_index("dp")
    share = width // (2 * contexts)
    tokens = tokens[0]
    cotangent = cotangent[0]
    query_up_t = query_up.T
    latent_down_t = latent_down.T
    gains = jnp.concatenate([attn_gain, mlp_gain, query_gain, latent_gain])[None]

    mine = lax.dynamic_slice_in_dim(group_order, 2 * z, 2)
    offsets = jnp.arange(HALF, dtype=jnp.int32)
    query_pos = (mine[:, None] * HALF + offsets[None, :]).reshape(rows)
    freq = 10000.0 ** (-2.0 * jnp.arange(ROPE // 2, dtype=F32) / ROPE)
    angle_t = freq[:, None] * query_pos.astype(F32)[None, :]
    cos_t, sin_t = jnp.cos(angle_t), jnp.sin(angle_t)

    (
        q_t,
        latent_all,
        latent_all_t,
        rope_all,
        rope_all_t,
        one_inverse,
        query_normed,
        query_inverse,
        query_t,
        cache_t,
        cache_inverse_t,
        one_t,
        feed_t,
        latent_up_t,
    ) = front(
        contexts,
        gains,
        tokens,
        cotangent,
        query_down,
        latent_down_t,
        query_up_t,
        latent_up,
        cos_t,
        sin_t,
    )
    joined_t, exact_t, lse = attention_forward(
        contexts, group_order, q_t, latent_all, latent_all_t, rope_all, latent_up, latent_up_t
    )
    (
        branch,
        two,
        hidden,
        dgate,
        dup,
        feed_part,
        dmiddle,
        dbranch,
        feed_all,
        far_two,
        far_dgate,
        near,
        dmix_t,
        mlp_gain_grad,
    ) = feed_forward(
        contexts,
        tensors,
        joined_t,
        tokens,
        cotangent,
        gains,
        attn_out,
        down_proj,
        gate_proj.T,
        up_proj.T,
        feed_t,
    )
    dq_t, lat_grad, dlat_t, grad_gate_proj, up_pieces, out_part, far_out, _, spread = backward(
        contexts,
        group_order,
        q_t,
        latent_all,
        latent_all_t,
        rope_all,
        rope_all_t,
        latent_up,
        latent_up_t,
        exact_t,
        lse,
        dmix_t,
        cos_t,
        sin_t,
        joined_t,
        two,
        far_two,
        dgate,
        far_dgate,
        dup,
        near,
        dbranch,
    )
    split = tensors
    while (share // split) % 16 != 0 or share % split != 0:
        split //= 2
    (
        norm_one,
        low_q,
        low_l,
        small_q,
        small_l,
        grad_attn_out,
        grad_up_proj,
        grad_down,
        gain_sums,
        feed,
    ) = tail(
        contexts,
        tensors,
        split,
        [
            dq_t.reshape(heads * (NOPE + ROPE), rows),
            query_up_t,
            query_t,
            query_normed,
            query_inverse,
            gains,
            dlat_t,
            cache_t,
            cache_inverse_t,
            cos_t,
            sin_t,
            lat_grad,
            one_inverse,
            mlp_gain_grad,
        ],
        [
            out_part,
            far_out,
            hidden,
            near,
            spread,
            feed_all,
            up_pieces,
            one_t,
            query_down,
            latent_down_t,
            tokens,
            feed_part,
        ],
    )
    (
        layer_out,
        token_grad,
        low_q,
        low_l,
        grad_gate_proj,
        grad_up_proj,
        grad_down,
        grad_attn_out,
        small_q,
        small_l,
    ) = finish(
        tokens,
        branch,
        feed,
        dmiddle,
        norm_one,
        low_q.reshape(share, -1),
        low_l.reshape(share, -1),
        [grad_gate_proj, grad_up_proj, grad_down, grad_attn_out, small_q, small_l],
    )

    gain_sums = gain_sums.reshape(-1)
    gain_grads = []
    edge = 0
    for value in (attn_gain, mlp_gain, query_gain, latent_gain):
        part = gain_sums[edge : edge + value.shape[0]].reshape(2 * contexts, -1)
        gain_grads.append(pick(part, d * contexts + z))
        edge += value.shape[0]

    return (
        layer_out[None],
        token_grad[None],
        gain_grads[0],
        low_q,
        gain_grads[2],
        low_l.T,
        gain_grads[3],
        small_q,
        small_l,
        grad_attn_out.T,
        gain_grads[1],
        grad_gate_proj,
        grad_up_proj,
        grad_down.T,
    )


def solution(mesh):
    in_specs = (
        P("dp", "context", None),
        P("dp", "context", None),
        P(),
        P(),
        P(),
        P(),
        P(),
        P(),
        P(None, "tensor"),
        P(None, "tensor"),
        P("tensor", None),
        P(),
        P(None, "tensor"),
        P(None, "tensor"),
        P("tensor", None),
    )
    out_specs = (
        P("dp", "context", None),
        P("dp", "context", None),
        P(("dp", "context")),
        P(("dp", "context"), None),
        P(("dp", "context")),
        P(("dp", "context"), None),
        P(("dp", "context")),
        P(("dp", "context"), "tensor"),
        P(("dp", "context"), "tensor"),
        P("tensor", ("dp", "context")),
        P(("dp", "context")),
        P(("dp", "context"), "tensor"),
        P(("dp", "context"), "tensor"),
        P("tensor", ("dp", "context")),
    )
    sizes = (mesh.shape["context"], mesh.shape["tensor"])
    return jax.shard_map(
        functools.partial(per_device, sizes),
        mesh=mesh,
        in_specs=in_specs,
        out_specs=out_specs,
        check_vma=False,
    )
```

profile of v0, /device:TPU:9, one launch (start us, length us, event | category | flops | bytes accessed | tf_op | source)
XLA Modules:
  0.0 424.8 jit_solution(11637309266736426952)
XLA Ops:
  0.7 0.7 dynamic-slice_multiply_fusion
  1.4 0.1 convert_bitcast_fusion
  1.5 1.4 pad_maximum_fusion
  2.8 0.8 multiply_sine_fusion
  3.7 28.8 %front.1 = (bf16[10,96,512]{2,1,0:T(8,128)(2,1)}, bf16[2048,256]{1,0:T(8,128)(2,1)}, bf16[256,2048]{1,0:T(8,128)(2,1)}, bf16[2048,128]{1,0:T(8,128)(2,1)}, bf16[...) custom-call(f32[1,6144]{1,0:T(1,128)} %bitcast.34, ...), custom_call_target="tpu_custom_call" | custom-call | flops 3145728000 | bytes 31457280 | tf_op jit(solution)/shard_map/front/pallas_call | solution.py:242
  32.4 28.9 %attention_forward.1 = (bf16[640,512]{1,0:T(8,128)(2,1)}, f32[10,64,512]{2,1,0:T(8,128)}, f32[10,1,512]{2,1,0:T(1,128)}) custom-call(s32[8]{0:T(128)} %order.3, bf16[10,96,512]{2,1,0:T(8,128)(2,1)} %get-tuple-element.73.q_t, bf16[2048,256]{1,0:T(8,128)(2,1)} %get-tuple-element.74.latent, bf16[256,2048]{1,0:T(8,128)(2,1)} %get-tuple-element.75.latent_t, ...), custom_call_target="tpu_custom_call" | custom-call | flops 8053063680 | bytes 12582912 | tf_op jit(solution)/shard_map/attention_forward/pallas_call | solution.py:404
  61.3 90.5 %feed_forward.1 = (bf16[512,2560]{1,0:T(8,128)(2,1)}, bf16[512,2560]{1,0:T(8,128)(2,1)}, bf16[512,1600]{1,0:T(8,128)(2,1)}, bf16[512,1600]{1,0:T(8,128)(2,1)}, b...) custom-call(bf16[640,512]{1,0:T(8,128)(2,1)} %get-tuple-element.78.j, ...), custom_call_target="tpu_custom_call" | custom-call | flops 25165824000 | bytes 62914560 | tf_op jit(solution)/shard_map/feed_forward/pallas_call | solution.py:864
  151.8 115.9 %backward.1 = (bf16[10,96,512]{2,1,0:T(8,128)(2,1)}, bf16[256,1280]{1,0:T(8,128)(2,1)}, bf16[288,2048]{1,0:T(8,128)(2,1)}, f32[320,1600]{1,0:T(8,128)}, bf16[128...) custom-call(s32[8]{0:T(128)} %order.3, ...), custom_call_target="tpu_custom_call" | custom-call | flops 20971520000 | bytes 41943040 | tf_op jit(solution)/shard_map/backward/pallas_call | solution.py:1345
  267.7 139.4 %tail.1 = (bf16[512,2560]{1,0:T(8,128)(2,1)}, bf16[4,80,768]{2,1,0:T(8,128)(2,1)}, bf16[4,80,288]{2,1,0:T(8,128)(2,1)}, f32[96,960]{1,0:T(8,128)}, f32[32,1280]{...) custom-call(bf16[960,512]{1,0:T(8,128)(2,1)} %bitcast.45, ...), custom_call_target="tpu_custom_call" | custom-call | flops 12582912000 | bytes 41943040 | tf_op jit(solution)/shard_map/tail/pallas_call | solution.py:2123
  407.1 0.0 copy-start
  407.1 15.2 %finish.1 = (bf16[512,2560]{1,0:T(8,128)(2,1)}, f32[512,2560]{1,0:T(8,128)}, f32[320,768]{1,0:T(8,128)}, f32[288,320]{1,0:T(8,128)}, f32[320,1600]{1,0:T(8,128)}...) custom-call(bf16[512,2560]{1,0:T(8,128)(2,1)} %bitcast.25, ...), custom_call_target="tpu_custom_call" | custom-call | tf_op jit(solution)/shard_map/finish/pallas_call | solution.py:2237
  422.3 0.0 copy-done
  422.4 0.1 reshape.79
  422.4 0.5 fusion
  423.0 0.1 reshape.80
  423.0 0.1 reshape.78
  423.1 0.6 dynamic-slice_reduce_fusion
  423.7 0.1 slice.17
  423.8 0.5 fusion.1
  (6 shorter events, 0.0 us)
Async XLA Ops:
  407.1 15.2 %copy-start = (f32[8,768]{1,0:T(8,128)S(1)}, f32[8,768]{1,0:T(8,128)}, u32[]{:S(2)}) copy-start(f32[8,768]{1,0:T(8,128)} %get-tuple-element.123) | copy-start | bytes 73732
where the time goes:
time: 431 us; the launch traced here: 425 us
  Pallas kernels  419 us (97%)
    pallas_call x1, Pallas kernels, tail(): pl.pallas_call(functools.partial(tail_kernel, contexts, tensors, split),...  139 us
    pallas_call x1, Pallas kernels, backward(): pl.pallas_call(functools.partial(backward_kernel, contexts, group), in_sp...  116 us
    pallas_call x1, Pallas kernels, feed_forward(): pl.pallas_call(functools.partial(feed_forward_kernel, contexts, tensors),...  90.5 us
    pallas_call x1, Pallas kernels, attention_forward(): pl.pallas_call(functools.partial(forward_kernel, heads, contexts), grid=(...  28.9 us
    pallas_call x1, Pallas kernels, front(): pl.pallas_call(functools.partial(front_kernel, contexts), in_specs=[insid...  28.8 us
    pallas_call x1, Pallas kernels, finish(): pl.pallas_call(functools.partial(finish_kernel, len(given)), grid=(steps,...  15.2 us

commit v1 on v0

--- a/solution.py
+++ b/solution.py
@@ -1820,9 +1820,9 @@
     q_back.start()
 
     feed_pair(0)
-    line_start(out_steps, out_far, out_got, 1, 2) if last >= 2 else None
     load_up.wait()
     line_start(up_steps, up_w, up_got, 2, 3) if last >= 3 else None
+    line_start(out_steps, out_far, out_got, 1, 2) if last >= 2 else None
     u_pair.wait_recv()
     l_pair.wait_recv()
 

time: 431 us -> 427 us (level)
  Pallas kernels: 419 us -> 413 us
    pallas_call x1, Pallas kernels: 28.9 us -> 15.2 us  [attention_forward(): pl.pallas_call(functools.partial(forward_kernel, heads, contexts), grid=(...]
    pallas_call x1, Pallas kernels: 90.5 us -> 103 us  [feed_forward(): pl.pallas_call(functools.partial(feed_forward_kernel, contexts, tensors),...]
    pallas_call x1, Pallas kernels: 139 us -> 134 us  [tail(): pl.pallas_call(functools.partial(tail_kernel, contexts, tensors, split),...]
where the time goes in v1:
time: 427 us; the launch traced here: 419 us
  Pallas kernels  413 us (97%)
    pallas_call x1, Pallas kernels, tail(): pl.pallas_call(functools.partial(tail_kernel, contexts, tensors, split),...  134 us
    pallas_call x1, Pallas kernels, backward(): pl.pallas_call(functools.partial(backward_kernel, contexts, group), in_sp...  117 us
    pallas_call x1, Pallas kernels, feed_forward(): pl.pallas_call(functools.partial(feed_forward_kernel, contexts, tensors),...  103 us
    pallas_call x1, Pallas kernels, front(): pl.pallas_call(functools.partial(front_kernel, contexts), in_specs=[insid...  28.8 us
    pallas_call x1, Pallas kernels, attention_forward(): pl.pallas_call(functools.partial(forward_kernel, heads, contexts), grid=(...  15.2 us
    pallas_call x1, Pallas kernels, finish(): pl.pallas_call(functools.partial(finish_kernel, len(given)), grid=(steps,...  15.2 us

profile of v1, /device:TPU:9, one launch (start us, length us, event | category | flops | bytes accessed | tf_op | source)
XLA Modules:
  0.0 419.4 jit_solution(12035438907337856668)
XLA Ops:
  0.7 0.7 dynamic-slice_multiply_fusion
  1.4 0.1 convert_bitcast_fusion
  1.5 1.4 pad_maximum_fusion
  2.8 0.8 multiply_sine_fusion
  3.7 28.8 %front.1 = (bf16[10,96,512]{2,1,0:T(8,128)(2,1)}, bf16[2048,256]{1,0:T(8,128)(2,1)}, bf16[256,2048]{1,0:T(8,128)(2,1)}, bf16[2048,128]{1,0:T(8,128)(2,1)}, bf16[...) custom-call(f32[1,6144]{1,0:T(1,128)} %bitcast.34, ...), custom_call_target="tpu_custom_call" | custom-call | flops 3145728000 | bytes 31457280 | tf_op jit(solution)/shard_map/front/pallas_call | solution.py:242
  32.4 15.2 %attention_forward.1 = (bf16[640,512]{1,0:T(8,128)(2,1)}, f32[10,64,512]{2,1,0:T(8,128)}, f32[10,1,512]{2,1,0:T(1,128)}) custom-call(s32[8]{0:T(128)} %order.3, bf16[10,96,512]{2,1,0:T(8,128)(2,1)} %get-tuple-element.73.q_t, bf16[2048,256]{1,0:T(8,128)(2,1)} %get-tuple-element.74.latent, bf16[256,2048]{1,0:T(8,128)(2,1)} %get-tuple-element.75.latent_t, ...), custom_call_target="tpu_custom_call" | custom-call | flops 8053063680 | bytes 12582912 | tf_op jit(solution)/shard_map/attention_forward/pallas_call | solution.py:404
  47.7 103.2 %feed_forward.1 = (bf16[512,2560]{1,0:T(8,128)(2,1)}, bf16[512,2560]{1,0:T(8,128)(2,1)}, bf16[512,1600]{1,0:T(8,128)(2,1)}, bf16[512,1600]{1,0:T(8,128)(2,1)}, b...) custom-call(bf16[640,512]{1,0:T(8,128)(2,1)} %get-tuple-element.78.j, ...), custom_call_target="tpu_custom_call" | custom-call | flops 25165824000 | bytes 62914560 | tf_op jit(solution)/shard_map/feed_forward/pallas_call | solution.py:864
  150.9 116.8 %backward.1 = (bf16[10,96,512]{2,1,0:T(8,128)(2,1)}, bf16[256,1280]{1,0:T(8,128)(2,1)}, bf16[288,2048]{1,0:T(8,128)(2,1)}, f32[320,1600]{1,0:T(8,128)}, bf16[128...) custom-call(s32[8]{0:T(128)} %order.3, ...), custom_call_target="tpu_custom_call" | custom-call | flops 20971520000 | bytes 41943040 | tf_op jit(solution)/shard_map/backward/pallas_call | solution.py:1345
  267.7 134.0 %tail.1 = (bf16[512,2560]{1,0:T(8,128)(2,1)}, bf16[4,80,768]{2,1,0:T(8,128)(2,1)}, bf16[4,80,288]{2,1,0:T(8,128)(2,1)}, f32[96,960]{1,0:T(8,128)}, f32[32,1280]{...) custom-call(bf16[960,512]{1,0:T(8,128)(2,1)} %bitcast.45, ...), custom_call_target="tpu_custom_call" | custom-call | flops 12582912000 | bytes 41943040 | tf_op jit(solution)/shard_map/tail/pallas_call | solution.py:2123
  401.7 0.0 copy-start
  401.7 15.2 %finish.1 = (bf16[512,2560]{1,0:T(8,128)(2,1)}, f32[512,2560]{1,0:T(8,128)}, f32[320,768]{1,0:T(8,128)}, f32[288,320]{1,0:T(8,128)}, f32[320,1600]{1,0:T(8,128)}...) custom-call(bf16[512,2560]{1,0:T(8,128)(2,1)} %bitcast.25, ...), custom_call_target="tpu_custom_call" | custom-call | tf_op jit(solution)/shard_map/finish/pallas_call | solution.py:2237
  416.9 0.0 copy-done
  416.9 0.1 reshape.79
  417.0 0.5 fusion
  417.5 0.1 reshape.80
  417.6 0.1 reshape.78
  417.6 0.6 dynamic-slice_reduce_fusion
  418.2 0.1 slice.17
  418.4 0.5 fusion.1
  (6 shorter events, 0.0 us)
Async XLA Ops:
  401.7 15.2 %copy-start = (f32[8,768]{1,0:T(8,128)S(1)}, f32[8,768]{1,0:T(8,128)}, u32[]{:S(2)}) copy-start(f32[8,768]{1,0:T(8,128)} %get-tuple-element.123) | copy-start | bytes 73732

commit v2 on v1

--- a/solution.py
+++ b/solution.py
@@ -1203,7 +1203,7 @@
 
     groups = heads // group
     total = groups * tiles
-    stops = [total * (i + 1) // (last + 1) for i in range(last)]
+    stops = [min(total, total * 5 * (i + 1) // (4 * (last + 1))) for i in range(last)]
 
     spread_start(2)
     for load in loads:

time: 427 us -> 427 us (level)
    pallas_call x1, Pallas kernels: 103 us -> 90.5 us  [feed_forward(): pl.pallas_call(functools.partial(feed_forward_kernel, contexts, tensors),...]
    pallas_call x1, Pallas kernels: 15.2 us -> 27.5 us  [attention_forward(): pl.pallas_call(functools.partial(forward_kernel, heads, contexts), grid=(...]
where the time goes in v2:
time: 427 us; the launch traced here: 418 us
  Pallas kernels  412 us (96%)
    pallas_call x1, Pallas kernels, tail(): pl.pallas_call(functools.partial(tail_kernel, contexts, tensors, split),...  134 us
    pallas_call x1, Pallas kernels, backward(): pl.pallas_call(functools.partial(backward_kernel, contexts, group), in_sp...  116 us
    pallas_call x1, Pallas kernels, feed_forward(): pl.pallas_call(functools.partial(feed_forward_kernel, contexts, tensors),...  90.5 us
    pallas_call x1, Pallas kernels, front(): pl.pallas_call(functools.partial(front_kernel, contexts), in_specs=[insid...  28.8 us
    pallas_call x1, Pallas kernels, attention_forward(): pl.pallas_call(functools.partial(forward_kernel, heads, contexts), grid=(...  27.5 us
    pallas_call x1, Pallas kernels, finish(): pl.pallas_call(functools.partial(finish_kernel, len(given)), grid=(steps,...  15.2 us

profile of v2, /device:TPU:9, one launch (start us, length us, event | category | flops | bytes accessed | tf_op | source)
XLA Modules:
  0.0 418.4 jit_solution(12215567596978813389)
XLA Ops:
  0.7 0.7 dynamic-slice_multiply_fusion
  1.4 0.1 convert_bitcast_fusion
  1.5 1.4 pad_maximum_fusion
  2.8 0.8 multiply_sine_fusion
  3.7 28.8 %front.1 = (bf16[10,96,512]{2,1,0:T(8,128)(2,1)}, bf16[2048,256]{1,0:T(8,128)(2,1)}, bf16[256,2048]{1,0:T(8,128)(2,1)}, bf16[2048,128]{1,0:T(8,128)(2,1)}, bf16[...) custom-call(f32[1,6144]{1,0:T(1,128)} %bitcast.34, ...), custom_call_target="tpu_custom_call" | custom-call | flops 3145728000 | bytes 31457280 | tf_op jit(solution)/shard_map/front/pallas_call | solution.py:242
  32.4 27.5 %attention_forward.1 = (bf16[640,512]{1,0:T(8,128)(2,1)}, f32[10,64,512]{2,1,0:T(8,128)}, f32[10,1,512]{2,1,0:T(1,128)}) custom-call(s32[8]{0:T(128)} %order.3, bf16[10,96,512]{2,1,0:T(8,128)(2,1)} %get-tuple-element.73.q_t, bf16[2048,256]{1,0:T(8,128)(2,1)} %get-tuple-element.74.latent, bf16[256,2048]{1,0:T(8,128)(2,1)} %get-tuple-element.75.latent_t, ...), custom_call_target="tpu_custom_call" | custom-call | flops 8053063680 | bytes 12582912 | tf_op jit(solution)/shard_map/attention_forward/pallas_call | solution.py:404
  60.0 90.5 %feed_forward.1 = (bf16[512,2560]{1,0:T(8,128)(2,1)}, bf16[512,2560]{1,0:T(8,128)(2,1)}, bf16[512,1600]{1,0:T(8,128)(2,1)}, bf16[512,1600]{1,0:T(8,128)(2,1)}, b...) custom-call(bf16[640,512]{1,0:T(8,128)(2,1)} %get-tuple-element.78.j, ...), custom_call_target="tpu_custom_call" | custom-call | flops 25165824000 | bytes 62914560 | tf_op jit(solution)/shard_map/feed_forward/pallas_call | solution.py:864
  150.5 115.9 %backward.1 = (bf16[10,96,512]{2,1,0:T(8,128)(2,1)}, bf16[256,1280]{1,0:T(8,128)(2,1)}, bf16[288,2048]{1,0:T(8,128)(2,1)}, f32[320,1600]{1,0:T(8,128)}, bf16[128...) custom-call(s32[8]{0:T(128)} %order.3, ...), custom_call_target="tpu_custom_call" | custom-call | flops 20971520000 | bytes 41943040 | tf_op jit(solution)/shard_map/backward/pallas_call | solution.py:1345
  266.4 134.4 %tail.1 = (bf16[512,2560]{1,0:T(8,128)(2,1)}, bf16[4,80,768]{2,1,0:T(8,128)(2,1)}, bf16[4,80,288]{2,1,0:T(8,128)(2,1)}, f32[96,960]{1,0:T(8,128)}, f32[32,1280]{...) custom-call(bf16[960,512]{1,0:T(8,128)(2,1)} %bitcast.45, ...), custom_call_target="tpu_custom_call" | custom-call | flops 12582912000 | bytes 41943040 | tf_op jit(solution)/shard_map/tail/pallas_call | solution.py:2123
  400.8 0.0 copy-start
  400.8 15.2 %finish.1 = (bf16[512,2560]{1,0:T(8,128)(2,1)}, f32[512,2560]{1,0:T(8,128)}, f32[320,768]{1,0:T(8,128)}, f32[288,320]{1,0:T(8,128)}, f32[320,1600]{1,0:T(8,128)}...) custom-call(bf16[512,2560]{1,0:T(8,128)(2,1)} %bitcast.25, ...), custom_call_target="tpu_custom_call" | custom-call | tf_op jit(solution)/shard_map/finish/pallas_call | solution.py:2237
  416.0 0.0 copy-done
  416.0 0.1 reshape.79
  416.1 0.5 fusion
  416.6 0.1 reshape.80
  416.7 0.1 reshape.78
  416.8 0.6 dynamic-slice_reduce_fusion
  417.4 0.1 slice.17
  417.5 0.5 fusion.1
  (6 shorter events, 0.0 us)
Async XLA Ops:
  400.8 15.2 %copy-start = (f32[8,768]{1,0:T(8,128)S(1)}, f32[8,768]{1,0:T(8,128)}, u32[]{:S(2)}) copy-start(f32[8,768]{1,0:T(8,128)} %get-tuple-element.123) | copy-start | bytes 73732
